TPU v7x, 32 devices: a whole 2x2x4 slice. The times are simulated.
32 devices in a mesh: groups: 2 (over y), domain: 4 (over z), band: 4 (over x, core).
Axes of the slice: x: 2, y: 2, z: 4, core: 2. Of those that a mesh axis runs over, the one named last changes fastest.
Arguments:
- orbitals: float32 [256, 32, 32, 128], P('band', 'domain', 'groups'), parts along dimension 2, may hold values from -48 to 48
- potential: float32 [32, 32, 128], P('domain', 'groups'), parts along dimension 1, may hold values from -1.5 to 0.5
- projector: float32 [48, 4, 256], P('domain', None, 'groups'), parts along dimension 2, may hold values from -0.5 to 0.5
- coupling: float32 [48, 8], P('domain', 'groups'), parts along dimension 1, may hold values from 1 to 4
- sphere_cells: int32 [48, 256], P('domain', 'groups'), parts along dimension 1, may hold values from 0 to 65535, as said below
- atom_count: int32 [8], P('groups'), parts along dimension 0, may hold values from 1 to 12, 32 in all
Outputs:
- filtered: float32 [256, 32, 32, 128], P('band', 'domain', 'groups'), parts along dimension 2
- gram: float32 [256, 512], P('band', 'groups'), parts along dimension 1
There are 2 independent parts, one for each index of `groups`. A program takes and returns all parts, laid end to end along the dimension named above; each array names one. Nothing has to cross between parts.
Inputs may be any that keep to these rules, and one draw needn't show every extreme that they name: `sphere_cells`: each atom slot a holds 128 distinct cells chosen within the cube of side 2 * 5 + 1 (periodically) around a center cell whose first coordinate lies in [8 (a // 12), 8 (a // 12 + 1)); a cell's flat index is (x 16 + y) * 128 + z.
All inputs are finite; a program needn't handle non-finite values.
Results may differ from a plain program's by a relative error of at most 0.0001.
Values sent between devices are 32-bit elements; how exact they have to be, the bound alone decides.
A program may use at most 192 MiB of HBM per device.

v0:
```python
import jax
import jax.numpy as jnp
from jax import lax
from jax.sharding import PartitionSpec as P

HALO = 6
SPH = 128


stencil_weights = (
    12.0 / 7.0,
    -15.0 / 56.0,
    10.0 / 189.0,
    -1.0 / 112.0,
    2.0 / 1925.0,
    -1.0 / 16632.0,
)
center_weight = -5369.0 / 1800.0
lower_edge = 2.0
upper_edge = 24.0
bottom_edge = -1.5


def padded_2(cells, sides, width):
    for axis, dim in sides:
        count = lax.axis_size(axis)
        head = lax.slice_in_dim(cells, 0, width, axis=dim)
        tail = lax.slice_in_dim(cells, cells.shape[dim] - width, cells.shape[dim], axis=dim)
        cells = jnp.concatenate(
            [
                lax.ppermute(tail, axis, [(i, (i + 1) % count) for i in range(count)]),
                cells,
                lax.ppermute(head, axis, [((i + 1) % count, i) for i in range(count)]),
            ],
            axis=dim,
        )
    return cells


def filter_scales():
    half_width = (upper_edge - lower_edge) / 2.0
    middle = (upper_edge + lower_edge) / 2.0
    ratio_first = half_width / (bottom_edge - middle)
    scales = [(ratio_first / half_width, 0.0)]
    ratio_next = 1.0 / (2.0 / ratio_first - ratio_first)
    scales.append((2.0 * ratio_next / half_width, ratio_first * ratio_next))
    return (middle, scales)


def weight_table(distance):
    table = jnp.where(distance == 0, center_weight, 0.0).astype(jnp.float32)
    for offset, weight in enumerate(stencil_weights, start=1):
        table = table + jnp.where(distance == offset, weight, 0.0).astype(jnp.float32)
    return table


def circulant(count):
    index = jnp.arange(count, dtype=jnp.int32)
    differ = (index[None, :] - index[:, None]) % count
    return weight_table(jnp.minimum(differ, count - differ))


def banded(slab):
    rows = jnp.arange(slab, dtype=jnp.int32)
    padded_rows = jnp.arange(slab + 2 * HALO, dtype=jnp.int32)
    return weight_table(jnp.abs(padded_rows[None, :] - HALO - rows[:, None]))


def per_device(orbitals, potential, projector, coupling, sphere_cells, atom_count):
    band_local, slab, rows_y, rows_z = orbitals.shape
    atom_slots = projector.shape[0]
    plane = rows_y * rows_z
    nx_total = slab * lax.axis_size("domain")
    domain_pos = lax.axis_index("domain")
    slab_start = domain_pos * slab
    live = (jnp.arange(atom_slots, dtype=jnp.int32) < atom_count[domain_pos]).astype(jnp.float32)
    strength = coupling * live[:, None]
    cell_x = sphere_cells // plane
    cell_rest = sphere_cells % plane
    gather_index = ((cell_x - slab_start + HALO) % nx_total * plane + cell_rest).reshape(-1)
    table_x = banded(slab)
    table_y = circulant(rows_y)
    table_z = circulant(rows_z)
    highest = lax.Precision.HIGHEST
    proj_all = padded_2(projector, (("domain", 0),), atom_slots)
    cells_all = padded_2(sphere_cells, (("domain", 0),), atom_slots)
    own_index = ((cells_all // plane - slab_start) % nx_total * plane + cells_all % plane).reshape(
        -1
    )

    def hamiltonian(current):
        padded = padded_2(current, (("domain", 1),), HALO)
        summed = jnp.einsum(
            "bpyz,ip->biyz", padded, table_x, precision=highest, preferred_element_type=jnp.float32
        )
        summed = summed + jnp.einsum(
            "bxyz,yw->bxwz", current, table_y, precision=highest, preferred_element_type=jnp.float32
        )
        summed = summed + jnp.einsum(
            "bxyz,zw->bxyw", current, table_z, precision=highest, preferred_element_type=jnp.float32
        )
        flattened = padded.reshape(band_local, -1)
        picked = flattened[:, gather_index].reshape(band_local, atom_slots, SPH)
        projection = jnp.einsum("ajs,bas->ajb", projector, picked, precision=highest)
        weighted = projection * strength[:, :, None]
        weights_all = padded_2(weighted, (("domain", 0),), atom_slots)
        images = jnp.einsum("ajs,ajb->bas", proj_all, weights_all, precision=highest)
        gathered_sum = jnp.zeros((band_local, slab * plane), jnp.float32)
        gathered_sum = gathered_sum.at[:, own_index].add(
            images.reshape(band_local, -1), mode="drop"
        )
        nonlocal_part = gathered_sum.reshape(band_local, slab, rows_y, rows_z)
        return -0.5 * summed + potential[None] * current + nonlocal_part

    middle, scales = filter_scales()
    previous = orbitals
    current = (hamiltonian(orbitals) - middle * orbitals) * scales[0][0]
    for scale_new, scale_old in scales[1:]:
        following = (hamiltonian(current) - middle * current) * scale_new - scale_old * previous
        previous, current = (current, following)
    cell_count = nx_total * plane
    spread_cells = lax.all_to_all(
        current.reshape(band_local, slab * plane), "band", split_axis=1, concat_axis=0, tiled=True
    )
    local_gram = jnp.dot(
        spread_cells, spread_cells.T, precision=highest, preferred_element_type=jnp.float32
    )
    whole_gram = lax.psum(local_gram, ("domain", "band"))
    gram_rows = lax.dynamic_slice_in_dim(
        whole_gram, lax.axis_index("band") * band_local, band_local, 0
    )
    return (current, gram_rows / cell_count)


def solution(mesh):
    placed = (
        P("band", "domain", "groups", None),
        P("domain", "groups", None),
        P("domain", None, "groups"),
        P("domain", "groups"),
        P("domain", "groups"),
        P("groups"),
    )
    return jax.shard_map(
        per_device,
        mesh=mesh,
        in_specs=placed,
        out_specs=(P("band", "domain", "groups", None), P("band", "groups")),
        check_vma=False,
    )
```

profile of v0, /device:TPU:1, one launch (start us, length us, event | category | flops | bytes accessed | tf_op | source)
XLA Modules:
  0.0 681.4 jit_solution(9572559535274063243)
XLA Ops:
  7.3 5.0 fusion.167
  12.2 2.1 collective-permute-start
  14.4 2.0 collective-permute-start.1
  16.4 3.3 collective-permute-start.3
  21.0 8.0 %fusion.49 = f32[16,64,8,128]{3,0,2,1:T(8,128)} fusion(f32[64,8,16,128]{3,2,1,0:T(8,128)} %param.6), kind=kOutput, calls=%fused_computation.97 | convolution fusion | flops 201335296 | bytes 8388608 | tf_op jit(solution)/shard_map/bxyz,yw->bxwz/dot_general | solution.py:96
  29.0 5.2 fusion.32
  34.8 3.9 copy.61
  39.5 112.1 %collective-permute-done.2 = s32[12,128]{1,0:T(8,128)S(1)} collective-permute-done((s32[12,128]{1,0:T(8,128)S(1)}, s32[12,128]{1,0:T(8,128)S(1)}, u32[]{:S(2)}, u32[]{:S(2)}) %collective-permute-start.2) | collective-permute-done | bytes 6176 | tf_op jit(solution)/shard_map/ppermute | solution.py:31
  152.0 0.9 fusion.38
  152.8 3.3 copy.60
  156.2 6.8 %copy.62 = f32[64,6,16,128]{3,1,2,0:T(8,128)} copy(f32[64,6,16,128]{3,2,1,0:T(8,128)} %collective-permute-done.1) | data formatting | bytes 6291456 | tf_op jit(solution)/shard_map/ppermute | solution.py:33
  163.0 10.6 %pad_maximum_fusion = f32[64,20,16,128]{3,1,2,0:T(8,128)} fusion(f32[64,6,16,128]{3,1,2,0:T(8,128)} %copy.62, f32[64,8,16,128]{3,1,2,0:T(8,128)} %copy.61, f32[64,6,16,128]{3,1,2,0:T(8,128)S(1)} %copy.60), kind=kLoop, calls=%fused_computation.4 | loop fusion | flops 5242880 | bytes 20971520 | tf_op jit(solution)/shard_map/concatenate | solution.py:29
  173.6 17.3 %copy.103 = f32[64,20,16,128]{0,3,2,1:T(8,128)} copy(f32[64,20,16,128]{3,1,2,0:T(8,128)} %pad_maximum_fusion) | data formatting | bytes 20971520 | tf_op jit(solution)/shard_map/reshape | solution.py:102
  190.9 9.5 %gather_fusion = f32[1536,64]{1,0:T(8,128)S(1)} fusion(f32[64,40960]{0,1:T(8,128)} %bitcast.133, s32[2048]{0:T(1024)S(1)} %pad_clamp_fusion), kind=kCustom, calls=%fused_computation | custom fusion | bytes 792576 | tf_op jit(solution)/shard_map/gather | solution.py:103
  200.5 0.8 fusion.18
  201.3 1.3 collective-permute-start.4
  202.6 2.0 collective-permute-start.5
  204.6 1.2 collective-permute-done.4
  205.8 2.0 convolution_bitcast_fusion.1
  207.9 0.9 copy.72
  208.8 29.3 %scatter_custom_fusion = f32[64,16384]{0,1:T(8,128)} fusion(s32[4608]{0:T(1024)} %fusion.38, f32[4608,64]{1,0:T(8,128)S(1)} %copy.72, f32[]{:T(128)} %constant.74.clone.1), kind=kCustom, calls=%fused_computation.24 | custom fusion | flops 294912 | bytes 4194816 | tf_op jit(solution)/shard_map/scatter-add | solution.py:109
  238.1 7.4 %copy.74 = f32[64,8,16,128]{3,1,2,0:T(8,128)} copy(f32[64,8,16,128]{0,3,2,1:T(8,128)} %bitcast.131) | data formatting | bytes 8388608 | tf_op jit(solution)/shard_map/reshape | solution.py:112
  245.5 18.6 %broadcast_multiply_fusion = (f32[64,8,16,128]{3,1,2,0:T(8,128)S(1)}, f32[64,8,16,128]{3,1,2,0:T(8,128)}) fusion(f32[64,8,16,128]{3,1,2,0:T(8,128)} %copy.74, f32[64,8,16,128]{3,2,1,0:T(8,128)} %param.6, f32[8,16,128]{2,0,1:T(8,128)S(1)} %copy-done.5, f32[128,64,8,16]{0,2,3,1:T(8,128)} %fusion.32, f32[16,64,8,128]{3,0,2,1:T(8,128)} %fusion.49, ...), kind=kOutput, calls=%fused_computation.26 | convolution fusion | flops 266341824 | bytes 35717200 | tf_op jit(solution)/shard_map/bpyz,ip->biyz/dot_general | solution.py:93
  264.1 1.0 fusion.166
  266.7 3.5 collective-permute-start.9
  270.8 5.1 fusion.11
  275.9 56.9 %collective-permute-done.8 = f32[64,6,16,128]{3,2,1,0:T(8,128)S(1)} collective-permute-done((f32[64,6,16,128]{3,2,1,0:T(8,128)S(1)}, f32[64,6,16,128]{3,2,1,0:T(8,128)S(1)}, u32[]{:S(2)}, u32[]{:S(2)}) %collective-permute-start.8) | collective-permute-done | bytes 3145760 | tf_op jit(solution)/shard_map/ppermute | solution.py:31
  332.9 3.5 copy.78
  336.4 66.9 %collective-permute-done.9 = f32[64,6,16,128]{3,2,1,0:T(8,128)S(1)} collective-permute-done((f32[64,6,16,128]{3,2,1,0:T(8,128)S(1)}, f32[64,6,16,128]{3,2,1,0:T(8,128)S(1)}, u32[]{:S(2)}, u32[]{:S(2)}) %collective-permute-start.9) | collective-permute-done | bytes 3145760 | tf_op jit(solution)/shard_map/ppermute | solution.py:33
  403.3 3.4 copy.79
  406.7 10.5 %pad_maximum_fusion.1 = f32[64,20,16,128]{3,1,2,0:T(8,128)} fusion(f32[64,6,16,128]{3,1,2,0:T(8,128)} %copy.79, f32[64,8,16,128]{3,1,2,0:T(8,128)S(1)} %get-tuple-element.12, f32[64,6,16,128]{3,1,2,0:T(8,128)} %copy.78), kind=kLoop, calls=%fused_computation.5 | loop fusion | flops 5242880 | bytes 20971520 | tf_op jit(solution)/shard_map/concatenate | solution.py:29
  417.3 17.3 %copy.106 = f32[64,20,16,128]{0,3,2,1:T(8,128)} copy(f32[64,20,16,128]{3,1,2,0:T(8,128)} %pad_maximum_fusion.1) | data formatting | bytes 20971520 | tf_op jit(solution)/shard_map/reshape | solution.py:102
  434.6 9.5 %gather_fusion.1 = f32[1536,64]{1,0:T(8,128)S(1)} fusion(f32[64,40960]{0,1:T(8,128)} %bitcast.132, s32[2048]{0:T(1024)S(1)} %pad_clamp_fusion), kind=kCustom, calls=%fused_computation.1 | custom fusion | bytes 792576 | tf_op jit(solution)/shard_map/gather | solution.py:103
  444.9 2.2 collective-permute-start.10
  447.2 1.3 collective-permute-start.11
  448.4 6.7 fusion.30
  455.1 2.0 convolution_bitcast_fusion
  457.3 0.9 copy.89
  458.1 29.1 %scatter_custom_fusion.1 = f32[64,16384]{0,1:T(8,128)} fusion(s32[4608]{0:T(1024)} %fusion.38, f32[4608,64]{1,0:T(8,128)S(1)} %copy.89, f32[]{:T(128)} %constant.74.clone.1), kind=kCustom, calls=%fused_computation.22 | custom fusion | flops 294912 | bytes 4194816 | tf_op jit(solution)/shard_map/scatter-add | solution.py:109
  487.3 7.4 %copy.91 = f32[64,8,16,128]{3,1,2,0:T(8,128)} copy(f32[64,8,16,128]{0,3,2,1:T(8,128)} %bitcast.130) | data formatting | bytes 8388608 | tf_op jit(solution)/shard_map/reshape | solution.py:112
  494.7 17.6 %fusion.6 = f32[64,8,16,128]{3,1,2,0:T(8,128)S(1)} fusion(f32[64,8,16,128]{3,1,2,0:T(8,128)} %copy.91, f32[64,8,16,128]{3,1,2,0:T(8,128)} %fusion.30, f32[16,64,8,128]{3,0,2,1:T(8,128)} %fusion.11, f32[64,8,16,128]{3,1,2,0:T(8,128)} %get-tuple-element.13, f32[8,16,128]{2,0,1:T(8,128)S(1)} %copy-done.6, s32[20]{0:T(128)S(1)} %copy-done.13, ...), kind=kOutput, calls=%fused_computation.13 | convolution fusion | flops 268438976 | bytes 35717200 | tf_op jit(solution)/shard_map/bpyz,ip->biyz/dot_general | solution.py:93
  512.3 2.9 copy.95
  515.2 5.3 all_to_all.14
  520.5 4.6 copy.94
  525.1 54.5 %all_to_all.19 = f32[64,4,4096]{2,0,1:T(8,128)S(1)} all-to-all(f32[64,4,4096]{2,0,1:T(8,128)S(1)} %copy.94), channel_id=1, replica_groups=mesh['groups'=2,'domain'=4,'band'=4] {'band'}, dimensions={1} | all-to-all | bytes 8388608 | tf_op jit(solution)/shard_map/all_to_all | solution.py:122
  579.6 4.2 fusion.168
  583.8 88.7 %all-reduce.2.cloned.1.call-done = f32[256,256]{1,0:T(8,128)} async-done(((f32[256,256]{1,0:T(8,128)}), f32[256,256]{1,0:T(8,128)}) %all-reduce.2.cloned.1.call-update) | async-done | bytes 262160 | tf_op jit(solution)/shard_map/psum | solution.py:128
  672.6 1.5 dynamic-slice_multiply_fusion
  (66 shorter events, 6.3 us)
Async XLA Ops:
  7.2 9.2 %copy-start.11 = (s32[12,128]{1,0:T(8,128)S(1)}, s32[12,128]{1,0:T(8,128)}, u32[]{:S(2)}) copy-start(s32[12,128]{1,0:T(8,128)} %param.10) | copy-start | bytes 18436
  7.2 12.5 %copy-start.9 = (f32[12,4,128]{2,1,0:T(4,128)S(1)}, f32[12,4,128]{2,1,0:T(4,128)}, u32[]{:S(2)}) copy-start(f32[12,4,128]{2,1,0:T(4,128)} %param.8) | copy-start | bytes 73732
  7.2 12.5 %copy-start.15 = (s32[4]{0:T(128)S(1)}, s32[4]{0:T(128)}, u32[]{:S(2)}) copy-start(s32[4]{0:T(128)} %param.11) | copy-start | bytes 52
  7.2 13.8 %copy-start.14 = (f32[12,4]{0,1:T(4,128)S(1)}, f32[12,4]{0,1:T(4,128)}, u32[]{:S(2)}) copy-start(f32[12,4]{0,1:T(4,128)} %param.9) | copy-start | bytes 580
  7.2 665.4 %all-reduce.2.cloned.1.call-start = ((), (), s32[]{:S(2)}) async-start(), calls=%async_computation.1 | async-start | bytes 524288 | tf_op jit(solution)/shard_map/psum | solution.py:128
  12.2 140.6 %collective-permute-start = (f32[64,6,16,128]{3,2,1,0:T(8,128)S(1)}, f32[64,6,16,128]{3,2,1,0:T(8,128)}, u32[]{:S(2)}, u32[]{:S(2)}) collective-permute-start(f32[64,6,16,128]{3,2,1,0:T(8,128)S(1)} %get-tuple-element.10), channel_id=1, source_target_pairs={{0,4},{4,8},{8,12},{12,0},{1,5},{5,9},{9,13},{13,1},{2,6},{6,10},{... | collective-permute-start | bytes 9437192 | tf_op jit(solution)/shard_map/ppermute | solution.py:31
  14.4 141.8 %collective-permute-start.1 = (f32[64,6,16,128]{3,2,1,0:T(8,128)}, f32[64,6,16,128]{3,2,1,0:T(8,128)}, u32[]{:S(2)}, u32[]{:S(2)}) collective-permute-start(f32[64,6,16,128]{3,2,1,0:T(8,128)} %get-tuple-element.11), channel_id=1, source_target_pairs={{4,0},{8,4},{12,8},{0,12},{5,1},{9,5},{13,9},{1,13},{6,2},{10,6},{... | collective-permute-start | bytes 9437192 | tf_op jit(solution)/shard_map/ppermute | solution.py:33
  16.4 135.2 %collective-permute-start.2 = (s32[12,128]{1,0:T(8,128)S(1)}, s32[12,128]{1,0:T(8,128)S(1)}, u32[]{:S(2)}, u32[]{:S(2)}) collective-permute-start(s32[12,128]{1,0:T(8,128)S(1)} %copy-done.11), channel_id=1, source_target_pairs={{0,4},{4,8},{8,12},{12,0},{1,5},{5,9},{9,13},{13,1},{2,6},{6,10},{... | collective-permute-start | bytes 18440 | tf_op jit(solution)/shard_map/ppermute | solution.py:31
  16.4 135.6 %collective-permute-start.3 = (s32[12,128]{1,0:T(8,128)S(1)}, s32[12,128]{1,0:T(8,128)S(1)}, u32[]{:S(2)}, u32[]{:S(2)}) collective-permute-start(s32[12,128]{1,0:T(8,128)S(1)} %copy-done.11), channel_id=1, source_target_pairs={{4,0},{8,4},{12,8},{0,12},{5,1},{9,5},{13,9},{1,13},{6,2},{10,6},{... | collective-permute-start | bytes 18440 | tf_op jit(solution)/shard_map/ppermute | solution.py:33
  19.6 133.2 %collective-permute-start.6 = (f32[12,4,128]{2,1,0:T(4,128)S(1)}, f32[12,4,128]{2,1,0:T(4,128)S(1)}, u32[]{:S(2)}, u32[]{:S(2)}) collective-permute-start(f32[12,4,128]{2,1,0:T(4,128)S(1)} %copy-done.9), channel_id=1, source_target_pairs={{0,4},{4,8},{8,12},{12,0},{1,5},{5,9},{9,13},{13,1},{2,6},{6,10},{... | collective-permute-start | bytes 73736 | tf_op jit(solution)/shard_map/ppermute | solution.py:31
  21.0 8.0 %copy-start.1 = (f32[64,8,16,128]{3,2,1,0:T(8,128)S(1)}, f32[64,8,16,128]{3,2,1,0:T(8,128)}, u32[]{:S(2)}) copy-start(f32[64,8,16,128]{3,2,1,0:T(8,128)} %param.6) | copy-start | bytes 12582916
  34.8 4.0 copy-start.7
  151.5 53.0 %collective-permute-start.7 = (f32[12,4,128]{2,1,0:T(4,128)S(1)}, f32[12,4,128]{2,1,0:T(4,128)S(1)}, u32[]{:S(2)}, u32[]{:S(2)}) collective-permute-start(f32[12,4,128]{2,1,0:T(4,128)S(1)} %copy-done.9), channel_id=1, source_target_pairs={{4,0},{8,4},{12,8},{0,12},{5,1},{9,5},{13,9},{1,13},{6,2},{10,6},{... | collective-permute-start | bytes 73736 | tf_op jit(solution)/shard_map/ppermute | solution.py:33
  156.2 6.9 %copy-start.2 = (f32[64,6,16,128]{3,1,2,0:T(8,128)}, f32[64,6,16,128]{3,1,2,0:T(8,128)S(1)}, u32[]{:S(2)}) copy-start(f32[64,6,16,128]{3,1,2,0:T(8,128)S(1)} %copy.60) | copy-start | bytes 9437188
  201.3 4.5 collective-permute-start.4
  202.6 3.2 collective-permute-start.5
  204.6 3.3 copy-start.3
  238.1 7.4 %copy-start.5 = (f32[8,16,128]{2,0,1:T(8,128)S(1)}, f32[8,16,128]{2,0,1:T(8,128)}, u32[]{:S(2)}) copy-start(f32[8,16,128]{2,0,1:T(8,128)} %copy.65) | copy-start | bytes 196612
  238.1 7.4 %copy-start.12 = (s32[20]{0:T(128)S(1)}, s32[20]{0:T(128)}, u32[]{:S(2)}) copy-start(s32[20]{0:T(128)} %iota_add_fusion) | copy-start | bytes 244
  264.1 142.6 %copy-start = (f32[64,8,16,128]{3,1,2,0:T(8,128)}, f32[64,8,16,128]{3,1,2,0:T(8,128)S(1)}, u32[]{:S(2)}) copy-start(f32[64,8,16,128]{3,1,2,0:T(8,128)S(1)} %get-tuple-element.12) | copy-start | bytes 12582916
  265.9 4.3 copy-start.8
  265.9 67.0 %collective-permute-start.8 = (f32[64,6,16,128]{3,2,1,0:T(8,128)S(1)}, f32[64,6,16,128]{3,2,1,0:T(8,128)S(1)}, u32[]{:S(2)}, u32[]{:S(2)}) collective-permute-start(f32[64,6,16,128]{3,2,1,0:T(8,128)S(1)} %copy.76), channel_id=1, source_target_pairs={{0,4},{4,8},{8,12},{12,0},{1,5},{5,9},{9,13},{13,1},{2,6},{6,10},{... | collective-permute-start | bytes 9437192 | tf_op jit(solution)/shard_map/ppermute | solution.py:31
  266.7 136.6 %collective-permute-start.9 = (f32[64,6,16,128]{3,2,1,0:T(8,128)S(1)}, f32[64,6,16,128]{3,2,1,0:T(8,128)S(1)}, u32[]{:S(2)}, u32[]{:S(2)}) collective-permute-start(f32[64,6,16,128]{3,2,1,0:T(8,128)S(1)} %copy.77), channel_id=1, source_target_pairs={{4,0},{8,4},{12,8},{0,12},{5,1},{9,5},{13,9},{1,13},{6,2},{10,6},{... | collective-permute-start | bytes 9437192 | tf_op jit(solution)/shard_map/ppermute | solution.py:33
  417.3 26.9 %copy-start.10 = (f32[12,4,128]{2,1,0:T(4,128)S(1)}, f32[12,4,128]{2,1,0:T(4,128)}, u32[]{:S(2)}) copy-start(f32[12,4,128]{2,1,0:T(4,128)} %param.8) | copy-start | bytes 73732
  444.9 10.2 %collective-permute-start.10 = (f32[12,4,64]{2,1,0:T(4,128)S(1)}, f32[12,4,64]{2,1,0:T(4,128)S(1)}, u32[]{:S(2)}, u32[]{:S(2)}) collective-permute-start(f32[12,4,64]{2,1,0:T(4,128)S(1)} %fusion.17), channel_id=1, source_target_pairs={{0,4},{4,8},{8,12},{12,0},{1,5},{5,9},{9,13},{13,1},{2,6},{6,10},{... | collective-permute-start | bytes 36872 | tf_op jit(solution)/shard_map/ppermute | solution.py:31
  447.2 8.0 %collective-permute-start.11 = (f32[12,4,64]{2,1,0:T(4,128)S(1)}, f32[12,4,64]{2,1,0:T(4,128)S(1)}, u32[]{:S(2)}, u32[]{:S(2)}) collective-permute-start(f32[12,4,64]{2,1,0:T(4,128)S(1)} %fusion.17), channel_id=1, source_target_pairs={{4,0},{8,4},{12,8},{0,12},{5,1},{9,5},{13,9},{1,13},{6,2},{10,6},{... | collective-permute-start | bytes 36872 | tf_op jit(solution)/shard_map/ppermute | solution.py:33
  448.4 6.7 copy-start.4
  487.3 7.4 %copy-start.6 = (f32[8,16,128]{2,0,1:T(8,128)S(1)}, f32[8,16,128]{2,0,1:T(8,128)}, u32[]{:S(2)}) copy-start(f32[8,16,128]{2,0,1:T(8,128)} %copy.84) | copy-start | bytes 196612
  487.3 7.4 %copy-start.13 = (s32[20]{0:T(128)S(1)}, s32[20]{0:T(128)}, u32[]{:S(2)}) copy-start(s32[20]{0:T(128)} %iota_add_fusion) | copy-start | bytes 244
Sparse Core Ops, SparseCore 0:
  584.0 88.5 all-reduce.1
where the time goes:
time: 689 us; the launch traced here: 681 us
  waiting for transfers between devices  326 us (47%)
  local copies, waits for them, and re-layouts  114 us (17%)
  other arithmetic  83.2 us (12%)
  matrix products  71.1 us (10%)
  blocking collectives  54.5 us (8%)
  starting transfers between devices  18 us (3%)
  between operations  14.9 us (2%)
    ppermute x6, waiting for transfers between devices, padded_2(): lax.ppermute(tail, axis, [(i, (i + 1) % count) for i in range(count)])  170 us
    psum x1, waiting for transfers between devices, per_device(): whole_gram = lax.psum(local_gram, ('domain', 'band'))  88.7 us
    ppermute x6, waiting for transfers between devices, padded_2(): lax.ppermute(head, axis, [((i + 1) % count, i) for i in range(count)])  67.1 us
    scatter-add x2, other arithmetic, hamiltonian(): gathered_sum.at[:, own_index]  58.4 us
    all_to_all x1, blocking collectives, per_device(): lax.all_to_all(current.reshape(band_local, slab * plane), 'band', split_a...  54.5 us
    dot_general x2, matrix products, hamiltonian(): jnp.einsum('bpyz,ip->biyz', padded, table_x, precision=highest, preferred...  36.2 us
    reshape x2, local copies, waits for them, and re-layouts, hamiltonian(): flattened = padded.reshape(band_local, -1)  34.6 us
    concatenate x2, other arithmetic, padded_2(): jnp.concatenate([lax.ppermute(tail, axis, [(i, (i + 1) % count) for i in...  21.1 us
  transfers between devices with their start and end apart: 13, of which 6 were waited for; matrix products, arithmetic and copies ran while one was open for 13% of the time, Pallas kernels for 0%

commit v1 on v0

v1 whole, which is shorter than its diff:
```python
import functools

import jax
import jax.numpy as jnp
from jax import lax
from jax.experimental import pallas as pl
from jax.experimental.pallas import tpu as pltpu
from jax.sharding import PartitionSpec as P

stencil_weights = (
    12.0 / 7.0,
    -15.0 / 56.0,
    10.0 / 189.0,
    -1.0 / 112.0,
    2.0 / 1925.0,
    -1.0 / 16632.0,
)
center_weight = -5369.0 / 1800.0
HALO = len(stencil_weights)
REACH = 5
MIDDLE = 13.0
HALF_WIDTH = 11.0
RATIO_1 = HALF_WIDTH / (-1.5 - MIDDLE)
RATIO_2 = 1.0 / (2.0 / RATIO_1 - RATIO_1)
SCALE_1 = RATIO_1 / HALF_WIDTH
SCALE_2 = 2.0 * RATIO_2 / HALF_WIDTH
SCALE_OLD = RATIO_1 * RATIO_2
VMEM = 56 * 1024 * 1024

NT = (((1,), (1,)), ((), ()))
NN = (((1,), (0,)), ((), ()))


def split(values):
    high = values.astype(jnp.bfloat16)
    low = (values - high.astype(jnp.float32)).astype(jnp.bfloat16)
    return high, low


def dot(a, b, dims):
    return lax.dot_general(a, b, dims, preferred_element_type=jnp.float32)


def dot3(a, b, dims):
    return dot(a[0], b[0], dims) + (dot(a[0], b[1], dims) + dot(a[1], b[0], dims))


def kinetic_weight(distance):
    table = jnp.where(distance == 0, -0.5 * center_weight, 0.0)
    for offset, weight in enumerate(stencil_weights, start=1):
        table = jnp.where(distance == offset, -0.5 * weight, table)
    return table


def periodic(difference, count):
    difference = jnp.abs(difference)
    return jnp.minimum(difference, count - difference)


def build_kernel(nx, ny, slab, x_ref, y_ref, z_ref, proj_ref, pot_ref, out_ref):
    rows = slab * ny
    nz = pot_ref.shape[-1]
    sph = proj_ref.shape[-1]
    row = lax.broadcasted_iota(jnp.int32, (rows, sph), 0)
    dx = periodic(row // ny - x_ref[0], nx)
    dy = periodic(row % ny - y_ref[0], ny)
    dz = periodic(lax.broadcasted_iota(jnp.int32, (nz, sph), 0) - z_ref[0], nz)
    same_x, same_y = dx == 0, dy == 0
    here = jnp.where(same_x & same_y, 1.0, 0.0)
    near = jnp.where(same_y, kinetic_weight(dx), 0.0) + jnp.where(same_x, kinetic_weight(dy), 0.0)
    point = jnp.where(dz == 0, 1.0, 0.0).astype(jnp.bfloat16)
    along_high, along_low = split(kinetic_weight(dz))
    none = jnp.zeros_like(point)
    right = jnp.concatenate(
        [jnp.concatenate([point, along_high], 1), jnp.concatenate([none, point], 1)], 0
    )
    fine = jnp.concatenate([none, along_low], 1)
    for j in range(proj_ref.shape[1]):
        values = proj_ref[0, j : j + 1, :]
        left = jnp.concatenate([near * values, here * values], 1)
        high, low = split(left)
        both = dot(high, right, NT) + dot(low, right, NT)
        plain = both[:, nz:]
        acted = both[:, :nz] + dot(high, fine, NT) + pot_ref[...] * plain
        flat = out_ref.reshape(rows * out_ref.shape[1], nz)
        nj = proj_ref.shape[1]
        flat[pl.ds(j, rows, stride=2 * nj), :] = acted
        flat[pl.ds(nj + j, rows, stride=2 * nj), :] = plain


def project_kernel(chunk, pq_ref, v_ref, out_ref, over_ref):
    @pl.when(pl.program_id(0) == 0)
    def _():
        out_ref[...] = jnp.zeros_like(out_ref)
        over_ref[...] = jnp.zeros_like(over_ref)

    bands, _, nz = v_ref.shape
    flat = v_ref.reshape(bands * chunk, nz)
    for r in range(0, chunk, 2):
        pq = jnp.concatenate([pq_ref[r], pq_ref[r + 1]], 1)
        v = jnp.concatenate(
            [flat[pl.ds(r, bands, stride=chunk), :], flat[pl.ds(r + 1, bands, stride=chunk), :]], 1
        )
        pq, v = split(pq), split(v)
        out_ref[...] += dot3(pq, v, NT)
        over_ref[...] += dot3(pq, pq, NT)


def local_kernel(v_ref, pot_ref, table_ref, out_ref, pad_ref, mid_ref):
    parts, _, slab, ny, nz = v_ref.shape
    nx = parts * slab
    step = 4
    table_high, table_low = split(table_ref[...])
    both_rows = jnp.concatenate([table_high, table_high], 0)

    def fill(read):
        for p in range(parts):
            pad_ref[pl.ds(HALO + p * slab, slab)] = read(p)
        pad_ref[pl.ds(0, HALO)] = pad_ref[pl.ds(nx, HALO)]
        pad_ref[pl.ds(HALO + nx, HALO)] = pad_ref[pl.ds(HALO, HALO)]

    def apply(start):
        center = pad_ref[pl.ds(HALO + start, step)]
        total = (-center_weight) * center
        for k, weight in enumerate(stencil_weights, start=1):
            around = (
                pad_ref[pl.ds(HALO + start + k, step)]
                + pad_ref[pl.ds(HALO + start - k, step)]
                + pltpu.roll(center, k, 1)
                + pltpu.roll(center, ny - k, 1)
            )
            total = total + (-0.5 * weight) * around
        high, low = split(center.reshape(step * ny, nz))
        along = dot(jnp.concatenate([high, low], 1), both_rows, NN) + dot(high, table_low, NN)
        total = total + along.reshape(step, ny, nz)
        return center, total + (pot_ref[pl.ds(start, step)] - MIDDLE) * center

    fill(lambda p: v_ref[p, 0])

    @pl.loop(0, nx // step)
    def _(i):
        _, acted = apply(i * step)
        mid_ref[pl.ds(i * step, step)] = SCALE_1 * acted

    fill(lambda p: mid_ref[pl.ds(p * slab, slab)])

    @pl.loop(0, nx // step)
    def _(i):
        _, acted = apply(i * step)
        each = slab // step
        p, q = i // each, i % each
        old = v_ref[p, 0, pl.ds(q * step, step)]
        out_ref[p, 0, pl.ds(q * step, step)] = SCALE_2 * acted - SCALE_OLD * old


def expand_kernel(chunk, pq_ref, coef_ref, y_ref, f_ref, g_ref):
    bands, _, nz = y_ref.shape
    coef = split(coef_ref[...])
    flat_y = y_ref.reshape(bands * chunk, nz)
    flat_f = f_ref.reshape(bands * chunk, nz)
    for r in range(chunk):
        total = dot3(coef, split(pq_ref[r]), NN) + flat_y[pl.ds(r, bands, stride=chunk), :]
        flat_f[pl.ds(r, bands, stride=chunk), :] = total
        g_ref[r] = total


def gram_kernel(chunk, x_ref, out_ref):
    @pl.when(pl.program_id(0) == 0)
    def _():
        out_ref[...] = jnp.zeros_like(out_ref)

    count, _, bands, nz = x_ref.shape
    for r in range(0, chunk, 2):
        x = jnp.concatenate(
            [x_ref[:, r].reshape(count * bands, nz), x_ref[:, r + 1].reshape(count * bands, nz)], 1
        )
        x = split(x)
        out_ref[...] += dot3(x, x, NT)


def call(kernel, **options):
    return pl.pallas_call(
        kernel, compiler_params=pltpu.CompilerParams(vmem_limit_bytes=VMEM), **options
    )


def per_device(orbitals, potential, projector, coupling, sphere_cells, atom_count):
    f32 = jnp.float32
    bands, slab, ny, nz = orbitals.shape
    slots, nj, sph = projector.shape
    nd, nb = lax.axis_size("domain"), lax.axis_size("band")
    nx, plane, rows = slab * nd, ny * nz, slab * ny
    pos = lax.axis_index("domain")
    share = bands // nd

    spread = lax.all_to_all(orbitals.reshape(nd, share, slab, ny, nz), "domain", 0, 0)
    pot_all = lax.all_gather(potential, "domain", axis=0, tiled=True)
    index = jnp.arange(nz, dtype=jnp.int32)
    table = kinetic_weight(periodic(index[:, None] - index[None, :], nz)).astype(f32)
    block = pl.BlockSpec((nd, 1, slab, ny, nz), lambda b: (0, b, 0, 0, 0))
    local = call(
        local_kernel,
        grid=(share,),
        in_specs=[
            block,
            pl.BlockSpec((nx, ny, nz), lambda b: (0, 0, 0)),
            pl.BlockSpec((nz, nz), lambda b: (0, 0)),
        ],
        out_specs=block,
        out_shape=jax.ShapeDtypeStruct(spread.shape, f32),
        scratch_shapes=[pltpu.VMEM((nx + 2 * HALO, ny, nz), f32), pltpu.VMEM((nx, ny, nz), f32)],
    )(spread, pot_all, table)
    local = lax.all_to_all(local, "domain", 0, 0).reshape(bands, rows, nz)

    near = -(-(REACH + HALO) // slab)
    proj_all = lax.all_gather(projector, "domain", axis=0, tiled=False)
    cells_all = lax.all_gather(sphere_cells, "domain", axis=0, tiled=False)
    coupling_all = lax.all_gather(coupling, "domain", axis=0, tiled=True)
    if nd <= 2 * near + 1:
        sources = jnp.arange(nd, dtype=jnp.int32)
    else:
        sources = (pos + jnp.arange(-near, near + 1, dtype=jnp.int32)) % nd
    atoms = sources.shape[0] * slots
    proj_near = proj_all[sources].reshape(atoms, nj, sph)
    cells = cells_all[sources].reshape(atoms, 1, sph)
    cell_x = (cells // plane - pos * slab) % nx
    per_atom = pl.BlockSpec((1, 1, sph), lambda a: (a, 0, 0))
    count = atoms * 2 * nj
    pq = call(
        functools.partial(build_kernel, nx, ny, slab),
        grid=(atoms,),
        in_specs=[
            per_atom,
            per_atom,
            per_atom,
            pl.BlockSpec((1, nj, sph), lambda a: (a, 0, 0)),
            pl.BlockSpec((rows, nz), lambda a: (0, 0)),
        ],
        out_specs=pl.BlockSpec((rows, 2 * nj, nz), lambda a: (0, a, 0)),
        out_shape=jax.ShapeDtypeStruct((rows, count, nz), f32),
    )(cell_x, cells // nz % ny, cells % nz, proj_near, potential.reshape(rows, nz))

    chunk = 8
    part_out, part_over = call(
        functools.partial(project_kernel, chunk),
        grid=(rows // chunk,),
        in_specs=[
            pl.BlockSpec((chunk, count, nz), lambda i: (i, 0, 0)),
            pl.BlockSpec((bands, chunk, nz), lambda i: (0, i, 0)),
        ],
        out_specs=[
            pl.BlockSpec((count, bands), lambda i: (0, 0)),
            pl.BlockSpec((count, count), lambda i: (0, 0)),
        ],
        out_shape=[
            jax.ShapeDtypeStruct((count, bands), f32),
            jax.ShapeDtypeStruct((count, count), f32),
        ],
    )(pq, orbitals.reshape(bands, rows, nz))
    width = atoms * nj
    part_out = part_out.reshape(atoms, 2, nj, bands)
    part_over = part_over.reshape(atoms, 2, nj, atoms, 2, nj)[:, 1, :, :, 1, :].reshape(width, width)
    parts = jnp.concatenate(
        [
            part_out[:, 0].reshape(width, bands),
            part_out[:, 1].reshape(width, bands),
        ],
        1,
    )
    total = nd * slots * nj
    if total != width:
        where = (sources[:, None] * (slots * nj) + jnp.arange(slots * nj)[None]).reshape(-1)
        parts = jnp.zeros((total, 2 * bands), f32).at[where].set(parts)
        part_over = jnp.zeros((total, total), f32).at[where[:, None], where[None, :]].set(part_over)
    summed = lax.psum(jnp.concatenate([parts, part_over], 1), "domain")
    acted, plain, over = (
        summed[:, :bands],
        summed[:, bands : 2 * bands],
        summed[:, 2 * bands :],
    )
    slot = jnp.arange(slots, dtype=jnp.int32)
    live = (slot[None, :] < atom_count[:, None]).reshape(-1)
    strength = jnp.where(live[:, None], coupling_all, 0.0).reshape(-1, 1)
    weight_0 = strength * plain
    plain_1 = SCALE_1 * (
        acted + jnp.dot(over, weight_0, precision=lax.Precision.HIGHEST) - MIDDLE * plain
    )
    coef_p = SCALE_2 * (strength * plain_1 - (MIDDLE * SCALE_1) * weight_0)
    coef_q = (SCALE_2 * SCALE_1) * weight_0
    coef = jnp.stack(
        [coef_q.reshape(nd, slots, nj, bands), coef_p.reshape(nd, slots, nj, bands)], 2
    )
    coef = coef[sources].reshape(count, bands).T

    filtered, shared = call(
        functools.partial(expand_kernel, chunk),
        grid=(rows // chunk,),
        in_specs=[
            pl.BlockSpec((chunk, count, nz), lambda i: (i, 0, 0)),
            pl.BlockSpec((bands, count), lambda i: (0, 0)),
            pl.BlockSpec((bands, chunk, nz), lambda i: (0, i, 0)),
        ],
        out_specs=[
            pl.BlockSpec((bands, chunk, nz), lambda i: (0, i, 0)),
            pl.BlockSpec((chunk, bands, nz), lambda i: (i, 0, 0)),
        ],
        out_shape=[
            jax.ShapeDtypeStruct((bands, rows, nz), f32),
            jax.ShapeDtypeStruct((rows, bands, nz), f32),
        ],
    )(pq, coef, local)

    shared = lax.all_to_all(shared.reshape(nb, rows // nb, bands, nz), "band", 0, 0)
    gram = call(
        functools.partial(gram_kernel, chunk),
        grid=(rows // nb // chunk,),
        in_specs=[pl.BlockSpec((nb, chunk, bands, nz), lambda i: (0, i, 0, 0))],
        out_specs=pl.BlockSpec((nb * bands, nb * bands), lambda i: (0, 0)),
        out_shape=jax.ShapeDtypeStruct((nb * bands, nb * bands), f32),
    )(shared)
    gram = lax.psum(gram, ("domain", "band"))
    gram = lax.dynamic_slice_in_dim(gram, lax.axis_index("band") * bands, bands, 0)
    return filtered.reshape(orbitals.shape), gram / (nx * plane)


def solution(mesh):
    placed = (
        P("band", "domain", "groups", None),
        P("domain", "groups", None),
        P("domain", None, "groups"),
        P("domain", "groups"),
        P("domain", "groups"),
        P("groups"),
    )
    return jax.shard_map(
        per_device,
        mesh=mesh,
        in_specs=placed,
        out_specs=(P("band", "domain", "groups", None), P("band", "groups")),
        check_vma=False,
    )
```

time: 689 us -> 655 us (0.951)
  blocking collectives: 54.5 us -> 268 us
  waiting for transfers between devices: 326 us -> 121 us
  Pallas kernels: 0 us -> 141 us
  other arithmetic: 83.2 us -> 5.57 us
  matrix products: 71.1 us -> 1.25 us
  local copies, waits for them, and re-layouts: 114 us -> 91 us
  starting transfers between devices: 18 us -> 10.6 us
    ppermute x12 -> x0, waiting for transfers between devices: 237 us -> none  [the longest x6 170 us: padded_2(): lax.ppermute(tail, axis, [(i, (i + 1) % count) for i in range(count)])]
    all_gather x0 -> x4, blocking collectives: none -> 213 us  [the longest x1 98.7 us: per_device(): pot_all = lax.all_gather(potential, 'domain', axis=0, tiled=True)]
    pallas_call x0 -> x5, Pallas kernels: none -> 141 us  [the longest x1 44.1 us: per_device(): call(local_kernel, grid=(share,), in_specs=[block, pl.BlockSpec((nx, ny,...]
    dot_general x11 -> x1, matrix products: 71.1 us -> 1.25 us  [per_device(): jnp.dot(over, weight_0, precision=lax.Precision.HIGHEST)]
    scatter-add x2 -> x0, other arithmetic: 58.4 us -> none  [hamiltonian(): gathered_sum.at[:, own_index]]
    slice x4 -> x2, local copies, waits for them, and re-layouts: 7.41 us -> 51.7 us  [the longest x1 50.8 us: per_device(): part_over.reshape(atoms, 2, nj, atoms, 2, nj)[:, 1, :, :, 1, :]]
    psum x1 -> x2, waiting for transfers between devices: 88.7 us -> 121 us  [the longest x1 88.9 us: per_device(): gram = lax.psum(gram, ('domain', 'band'))]
    concatenate x2 -> x1, other arithmetic: 21.1 us -> 0.78 us  [per_device(): summed = lax.psum(jnp.concatenate([parts, part_over], 1), 'domain')]
  transfers between devices with their start and end apart: 13 -> 4, of which waited for: 6 -> 2; matrix products, arithmetic and copies ran while one was open for 13% -> 15% of each run, Pallas kernels for 0% -> 11%
where the time goes in v1:
time: 655 us; the launch traced here: 653 us
  blocking collectives  268 us (41%)
  Pallas kernels  141 us (22%)
  waiting for transfers between devices  121 us (18%)
  local copies, waits for them, and re-layouts  91 us (14%)
  between operations  14.2 us (2%)
  starting transfers between devices  10.6 us (2%)
    all_gather x1, blocking collectives, per_device(): pot_all = lax.all_gather(potential, 'domain', axis=0, tiled=True)  98.7 us
    all_gather x1, blocking collectives, per_device(): cells_all = lax.all_gather(sphere_cells, 'domain', axis=0, tiled=False)  94.8 us
    psum x1, waiting for transfers between devices, per_device(): gram = lax.psum(gram, ('domain', 'band'))  88.9 us
    all_to_all x1, blocking collectives, per_device(): lax.all_to_all(shared.reshape(nb, rows // nb, bands, nz), 'band', 0, 0)  55 us
    slice x1, local copies, waits for them, and re-layouts, per_device(): part_over.reshape(atoms, 2, nj, atoms, 2, nj)[:, 1, :, :, 1, :]  50.8 us
    pallas_call x1, Pallas kernels, per_device(): call(local_kernel, grid=(share,), in_specs=[block, pl.BlockSpec((nx, ny,...  44.1 us
    pallas_call x1, Pallas kernels, per_device(): call(functools.partial(build_kernel, nx, ny, slab), grid=(atoms,), in_spe...  36.6 us
    pallas_call x1, Pallas kernels, per_device(): call(functools.partial(project_kernel, chunk), grid=(rows // chunk,), in_...  34.6 us
  transfers between devices with their start and end apart: 4, of which 2 were waited for; matrix products, arithmetic and copies ran while one was open for 15% of the time, Pallas kernels for 11%

profile of v1, /device:TPU:1, one launch (start us, length us, event | category | flops | bytes accessed | tf_op | source)
XLA Modules:
  0.0 652.7 jit_solution(11324425735901591085)
XLA Ops:
  7.2 0.0 copy-start
  7.2 5.6 all-to-all-start
  12.7 98.7 %all_gather.23.pot_ref = f32[32,16,128]{2,1,0:T(8,128)} all-gather(f32[8,16,128]{2,1,0:T(8,128)S(1)} %copy-done), channel_id=1, replica_groups=mesh['groups'=2,'domain'=4,'band'=4] {'domain'}, dimensions={0}, use_global_device_ids=true | all-gather | bytes 327680 | tf_op jit(solution)/shard_map/all_gather | solution.py:197
  111.4 0.7 select_select_fusion.table_ref
  112.1 0.0 all-to-all-done.v_ref
  112.1 44.1 %shard_map.79 = f32[4,16,8,16,128]{4,3,2,1,0:T(8,128)} custom-call(f32[4,16,8,16,128]{4,3,2,1,0:T(8,128)} %all-to-all-done.v_ref, f32[32,16,128]{2,1,0:T(8,128)} %all_gather.23.pot_ref, f32[128,128]{1,0:T(8,128)} %select_select_fusion.table_ref), custom_call_target="tpu_custom_call" | custom-call | tf_op jit(solution)/shard_map/pallas_call | solution.py:201
  156.3 5.0 all-to-all-start.1
  161.3 0.0 all-reduce.3.cloned.1.call-start
  161.3 94.8 %all-gather.2 = s32[4,12,128]{2,1,0:T(8,128)S(1)} all-gather(s32[1,12,128]{2,1,0:T(8,128)S(1)} %bitcast.48), channel_id=2, replica_groups=mesh['groups'=2,'domain'=4,'band'=4] {'domain'}, dimensions={0}, use_global_device_ids=true | all-gather | bytes 30720 | tf_op jit(solution)/shard_map/all_gather | solution.py:217
  256.2 0.5 gather_fusion
  256.7 10.6 %all-gather.1 = f32[48,4,128]{2,1,0:T(4,128)S(1)} all-gather(f32[12,4,128]{2,1,0:T(4,128)S(1)} %copy-done.1), channel_id=3, replica_groups=mesh['groups'=2,'domain'=4,'band'=4] {'domain'}, dimensions={0}, use_global_device_ids=true | all-gather | bytes 122880 | tf_op jit(solution)/shard_map/all_gather | solution.py:216
  267.4 1.2 gather_fusion.1
  268.6 0.7 and_select_fusion
  269.3 0.9 and_select_fusion.1
  270.2 36.6 %shard_map.77.pq_ref = f32[128,384,128]{2,1,0:T(8,128)} custom-call(s32[48,1,128]{2,1,0:T(1,128)} %get-tuple-element.15.x_ref, s32[48,1,128]{2,1,0:T(1,128)} %get-tuple-element.14.y_ref, s32[48,1,128]{2,1,0:T(1,128)} %get-tuple-element.10.z_ref, f32[48,4,128]{2,1,0:T(4,128)} %bitcast.37, f32[128,128]{1,0:T(8,128)} %bitcast.44), custom_call_target="tpu_custom_call" | custom-call | tf_op jit(solution)/shard_map/pallas_call | solution.py:229
  306.8 34.6 %shard_map.78 = (f32[384,64]{1,0:T(8,128)}, f32[384,384]{1,0:T(8,128)}) custom-call(f32[128,384,128]{2,1,0:T(8,128)} %shard_map.77.pq_ref, f32[64,128,128]{2,1,0:T(8,128)} %bitcast.34), custom_call_target="tpu_custom_call" | custom-call | tf_op jit(solution)/shard_map/pallas_call | solution.py:244
  341.4 1.0 fusion.16
  342.4 0.1 copy.35
  342.5 0.1 copy.36
  342.6 31.4 %reshape.353 = f32[48,2,4,48,2,4]{5,4,3,2,1,0:T(2,128)} reshape(f32[384,384]{1,0:T(8,128)} %get-tuple-element.7) | data formatting | bytes 1179648 | tf_op jit(solution)/shard_map/reshape | solution.py:262
  374.0 50.8 %slice_reduce_fusion = f32[48,4,48,4]{3,2,1,0:T(8,128)} fusion(f32[48,2,4,48,2,4]{5,4,3,2,1,0:T(2,128)} %reshape.353), kind=kLoop, calls=%fused_computation.3 | loop fusion | bytes 294912 | tf_op jit(solution)/shard_map/slice | solution.py:262
  424.8 3.8 reshape_squeeze.11
  428.6 0.1 copy.37
  428.7 0.8 pad_maximum_fusion
  429.5 0.0 all-reduce.3.cloned.1.call-update
  429.5 0.0 all-reduce.5.cloned.1.call-start
  429.5 0.0 copy-done.3
  429.6 9.3 %all-gather.3 = f32[4,12,4]{1,2,0:T(4,128)S(1)} all-gather(f32[1,12,4]{1,2,0:T(4,128)S(1)} %bitcast.49), channel_id=1, replica_groups=mesh['groups'=2,'domain'=4,'band'=4] {'domain'}, dimensions={0}, use_global_device_ids=true | all-gather | bytes 960 | tf_op jit(solution)/shard_map/all_gather | solution.py:218
  438.9 0.1 reshape.388
  438.9 0.1 iota_compare_fusion
  439.0 0.1 lt.46
  439.1 0.1 copy.32
  439.2 0.1 mul.55
  439.3 32.0 %all-reduce.3.cloned.1.call-done = f32[192,320]{0,1:T(8,128)} async-done(((f32[192,320]{0,1:T(8,128)}), f32[192,320]{0,1:T(8,128)}) %all-reduce.3.cloned.1.call-update) | async-done | bytes 245776 | tf_op jit(solution)/shard_map/psum | solution.py:275
  471.3 1.2 fusion.3
  472.6 0.1 copy.39
  472.7 0.9 fusion.12
  473.5 0.1 copy.38
  473.6 0.1 pad_maximum_fusion.1
  473.7 0.7 gather_fusion.2
  474.3 0.8 copy.42
  475.1 0.0 all-to-all-done.1
  475.1 20.3 %shard_map.80 = (f32[64,128,128]{2,1,0:T(8,128)}, f32[128,64,128]{2,1,0:T(8,128)}) custom-call(f32[128,384,128]{2,1,0:T(8,128)} %shard_map.77.pq_ref, f32[64,384]{1,0:T(8,128)} %bitcast.43, f32[64,128,128]{2,1,0:T(8,128)} %bitcast.20.y_ref), custom_call_target="tpu_custom_call" | custom-call | tf_op jit(solution)/shard_map/pallas_call | solution.py:295
  495.4 55.0 %all_to_all.15.x_ref = f32[4,32,64,128]{3,2,1,0:T(8,128)} all-to-all(f32[4,32,64,128]{3,2,1,0:T(8,128)} %bitcast.35), channel_id=1, replica_groups=mesh['groups'=2,'domain'=4,'band'=4] {'band'}, dimensions={0} | all-to-all | bytes 8388608 | tf_op jit(solution)/shard_map/all_to_all | solution.py:313
  550.3 5.1 shard_map.81
  555.5 0.0 all-reduce.5.cloned.1.call-update
  555.5 88.9 %all-reduce.5.cloned.1.call-done = f32[256,256]{1,0:T(8,128)} async-done(((f32[256,256]{1,0:T(8,128)}), f32[256,256]{1,0:T(8,128)}) %all-reduce.5.cloned.1.call-update) | async-done | bytes 262160 | tf_op jit(solution)/shard_map/psum | solution.py:321
  644.4 1.5 dynamic-slice_multiply_fusion
  (14 shorter events, 0.0 us)
Async XLA Ops:
  7.2 5.6 copy-start
  7.2 105.0 %all-to-all-start = ((f32[4,16,8,16,128]{4,3,2,1,0:T(8,128)}), f32[4,16,8,16,128]{4,3,2,1,0:T(8,128)}, u32[]{:S(2)}, u32[]{:S(2)}) async-start(f32[4,16,8,16,128]{4,3,2,1,0:T(8,128)} %bitcast.33), calls=%async_computation | async-start | bytes 8388608 | tf_op jit(solution)/shard_map/all_to_all | solution.py:196
  156.3 5.1 copy-start.2
  156.3 100.5 %copy-start.1 = (f32[12,4,128]{2,1,0:T(4,128)S(1)}, f32[12,4,128]{2,1,0:T(4,128)}, u32[]{:S(2)}) copy-start(f32[12,4,128]{2,1,0:T(4,128)} %param.8) | copy-start | bytes 73732
  156.3 318.8 %all-to-all-start.1 = ((f32[4,16,8,16,128]{4,3,2,1,0:T(8,128)}), f32[4,16,8,16,128]{4,3,2,1,0:T(8,128)}, u32[]{:S(2)}, u32[]{:S(2)}) async-start(f32[4,16,8,16,128]{4,3,2,1,0:T(8,128)} %shard_map.79), calls=%async_computation.1 | async-start | bytes 8388608 | tf_op jit(solution)/shard_map/all_to_all | solution.py:213
  161.3 310.0 %all-reduce.3.cloned.1.call-start = ((), (), s32[]{:S(2)}) async-start(), calls=%async_computation.3 | async-start | bytes 655360 | tf_op jit(solution)/shard_map/psum | solution.py:275
  424.8 4.8 copy-start.3
  424.8 14.2 %copy-start.4 = (s32[4]{0:T(128)S(1)}, s32[4]{0:T(128)}, u32[]{:S(2)}) copy-start(s32[4]{0:T(128)} %param.11) | copy-start | bytes 52
  429.5 214.9 %all-reduce.5.cloned.1.call-start = ((), (), s32[]{:S(2)}) async-start(), calls=%async_computation.4 | async-start | bytes 524288 | tf_op jit(solution)/shard_map/psum | solution.py:321
Sparse Core Ops, SparseCore 0:
  429.6 41.6 all-reduce.2
  555.6 88.7 all-reduce.4

commit v2 on v1

--- a/solution.py
+++ b/solution.py
@@ -106,8 +106,10 @@
         over_ref[...] += dot3(pq, pq, NT)
 
 
-def local_kernel(v_ref, pot_ref, table_ref, out_ref, pad_ref, mid_ref):
-    parts, _, slab, ny, nz = v_ref.shape
+def local_kernel(parts, *refs):
+    v_refs, (pot_ref, table_ref) = refs[:parts], refs[parts : parts + 2]
+    out_refs, (pad_ref, mid_ref) = refs[parts + 2 : 2 * parts + 2], refs[2 * parts + 2 :]
+    _, slab, ny, nz = v_refs[0].shape
     nx = parts * slab
     step = 4
     table_high, table_low = split(table_ref[...])
@@ -133,49 +135,84 @@
         high, low = split(center.reshape(step * ny, nz))
         along = dot(jnp.concatenate([high, low], 1), both_rows, NN) + dot(high, table_low, NN)
         total = total + along.reshape(step, ny, nz)
-        return center, total + (pot_ref[pl.ds(start, step)] - MIDDLE) * center
-
-    fill(lambda p: v_ref[p, 0])
+        return total + (pot_ref[pl.ds(start, step)] - MIDDLE) * center
+
+    fill(lambda p: v_refs[p][0])
 
     @pl.loop(0, nx // step)
     def _(i):
-        _, acted = apply(i * step)
-        mid_ref[pl.ds(i * step, step)] = SCALE_1 * acted
+        mid_ref[pl.ds(i * step, step)] = SCALE_1 * apply(i * step)
 
     fill(lambda p: mid_ref[pl.ds(p * slab, slab)])
 
-    @pl.loop(0, nx // step)
-    def _(i):
-        _, acted = apply(i * step)
-        each = slab // step
-        p, q = i // each, i % each
-        old = v_ref[p, 0, pl.ds(q * step, step)]
-        out_ref[p, 0, pl.ds(q * step, step)] = SCALE_2 * acted - SCALE_OLD * old
-
-
-def expand_kernel(chunk, pq_ref, coef_ref, y_ref, f_ref, g_ref):
-    bands, _, nz = y_ref.shape
+    for p in range(parts):
+
+        @pl.loop(0, slab // step)
+        def _(i, p=p):
+            old = v_refs[p][0, pl.ds(i * step, step)]
+            acted = apply(p * slab + i * step)
+            out_refs[p][0, pl.ds(i * step, step)] = SCALE_2 * acted - SCALE_OLD * old
+
+
+def expand_kernel(chunk, parts, halves, pos_ref, pq_ref, coef_ref, *refs):
+    y_refs, (f_ref, g_ref) = refs[: parts * halves], refs[parts * halves :]
+    each, _, nz = y_refs[0].shape
+    bands = f_ref.shape[0]
+    flat_y = [y_ref.reshape(each * chunk, nz) for y_ref in y_refs]
+    flat_f = f_ref.reshape(bands * chunk, nz)
     coef = split(coef_ref[...])
-    flat_y = y_ref.reshape(bands * chunk, nz)
-    flat_f = f_ref.reshape(bands * chunk, nz)
     for r in range(chunk):
-        total = dot3(coef, split(pq_ref[r]), NN) + flat_y[pl.ds(r, bands, stride=chunk), :]
-        flat_f[pl.ds(r, bands, stride=chunk), :] = total
-        g_ref[r] = total
-
-
-def gram_kernel(chunk, x_ref, out_ref):
+        added = dot3(coef, split(pq_ref[r]), NN)
+        for p in range(parts):
+            for h in range(halves):
+                first = (p * halves + h) * each
+                total = (
+                    added[first : first + each]
+                    + flat_y[p * halves + h][pl.ds(r, each, stride=chunk), :]
+                )
+                to = lax.rem(pos_ref[0] + p, parts) * (halves * each) + h * each
+                flat_f[pl.ds(to * chunk + r, each, stride=chunk), :] = total
+                g_ref[r, pl.ds(pl.multiple_of(to, each), each), :] = total
+
+
+def gram_kernel(chunk, count, pos_ref, *refs):
+    x_refs, (out_ref, x_scratch) = refs[:count], refs[count:]
+
     @pl.when(pl.program_id(0) == 0)
     def _():
         out_ref[...] = jnp.zeros_like(out_ref)
 
-    count, _, bands, nz = x_ref.shape
+    _, bands, nz = x_refs[0].shape
     for r in range(0, chunk, 2):
-        x = jnp.concatenate(
-            [x_ref[:, r].reshape(count * bands, nz), x_ref[:, r + 1].reshape(count * bands, nz)], 1
-        )
-        x = split(x)
+        for p in range(count):
+            at = pl.multiple_of(lax.rem(pos_ref[0] + count - p, count) * bands, bands)
+            x_scratch[pl.ds(at, bands), :] = jnp.concatenate([x_refs[p][r], x_refs[p][r + 1]], 1)
+        x = split(x_scratch[...])
         out_ref[...] += dot3(x, x, NT)
+
+
+def shifted(values, axis, by):
+    count = lax.axis_size(axis)
+    return lax.ppermute(values, axis, [(i, (i + by) % count) for i in range(count)])
+
+
+def summed_over(values, axis):
+    count = lax.axis_size(axis)
+    if count > 8:
+        return lax.psum(values, axis)
+    total = values
+    for p in range(1, count):
+        total = total + shifted(values, axis, p)
+    return total
+
+
+def block_of(values, index, count):
+    size = values.shape[0] // count
+    return lax.dynamic_slice_in_dim(values, index % count * size, size, 0)
+
+
+def cost(flops, moved):
+    return pl.CostEstimate(flops=flops, bytes_accessed=moved, transcendentals=0)
 
 
 def call(kernel, **options):
@@ -192,25 +229,42 @@
     nx, plane, rows = slab * nd, ny * nz, slab * ny
     pos = lax.axis_index("domain")
     share = bands // nd
-
-    spread = lax.all_to_all(orbitals.reshape(nd, share, slab, ny, nz), "domain", 0, 0)
+    halves = 2 if share % 2 == 0 else 1
+    each = share // halves
+
     pot_all = lax.all_gather(potential, "domain", axis=0, tiled=True)
+    pot_all = lax.dynamic_slice_in_dim(
+        jnp.concatenate([pot_all, pot_all], 0), pos * slab, nx, 0
+    )
     index = jnp.arange(nz, dtype=jnp.int32)
     table = kinetic_weight(periodic(index[:, None] - index[None, :], nz)).astype(f32)
-    block = pl.BlockSpec((nd, 1, slab, ny, nz), lambda b: (0, b, 0, 0, 0))
-    local = call(
-        local_kernel,
-        grid=(share,),
-        in_specs=[
-            block,
-            pl.BlockSpec((nx, ny, nz), lambda b: (0, 0, 0)),
-            pl.BlockSpec((nz, nz), lambda b: (0, 0)),
-        ],
-        out_specs=block,
-        out_shape=jax.ShapeDtypeStruct(spread.shape, f32),
-        scratch_shapes=[pltpu.VMEM((nx + 2 * HALO, ny, nz), f32), pltpu.VMEM((nx, ny, nz), f32)],
-    )(spread, pot_all, table)
-    local = lax.all_to_all(local, "domain", 0, 0).reshape(bands, rows, nz)
+    block = pl.BlockSpec((1, slab, ny, nz), lambda b: (b, 0, 0, 0))
+
+    def sent(h, p):
+        start = (pos - p) % nd * share + h * each
+        part = lax.dynamic_slice_in_dim(orbitals, start, each, 0)
+        return shifted(part, "domain", -p) if p else part
+
+    local = []
+    for h in range(halves):
+        spread = [sent(h, p) for p in range(nd)]
+        results = call(
+            functools.partial(local_kernel, nd),
+            grid=(each,),
+            in_specs=[block] * nd
+            + [
+                pl.BlockSpec((nx, ny, nz), lambda b: (0, 0, 0)),
+                pl.BlockSpec((nz, nz), lambda b: (0, 0)),
+            ],
+            out_specs=[block] * nd,
+            out_shape=[jax.ShapeDtypeStruct(spread[0].shape, f32)] * nd,
+            scratch_shapes=[
+                pltpu.VMEM((nx + 2 * HALO, ny, nz), f32),
+                pltpu.VMEM((nx, ny, nz), f32),
+            ],
+            cost_estimate=cost(share * nx * plane * 6000, share * nx * plane * 4),
+        )(*spread, pot_all, table)
+        local.append([shifted(part, "domain", p) if p else part for p, part in enumerate(results)])
 
     near = -(-(REACH + HALO) // slab)
     proj_all = lax.all_gather(projector, "domain", axis=0, tiled=False)
@@ -238,6 +292,7 @@
         ],
         out_specs=pl.BlockSpec((rows, 2 * nj, nz), lambda a: (0, a, 0)),
         out_shape=jax.ShapeDtypeStruct((rows, count, nz), f32),
+        cost_estimate=cost(atoms * 600_000_000, rows * count * nz * 4),
     )(cell_x, cells // nz % ny, cells % nz, proj_near, potential.reshape(rows, nz))
 
     chunk = 8
@@ -256,50 +311,61 @@
             jax.ShapeDtypeStruct((count, bands), f32),
             jax.ShapeDtypeStruct((count, count), f32),
         ],
+        cost_estimate=cost(rows * nz * count * (count + bands) * 8, rows * count * nz * 4),
     )(pq, orbitals.reshape(bands, rows, nz))
-    width = atoms * nj
-    part_out = part_out.reshape(atoms, 2, nj, bands)
-    part_over = part_over.reshape(atoms, 2, nj, atoms, 2, nj)[:, 1, :, :, 1, :].reshape(width, width)
-    parts = jnp.concatenate(
-        [
-            part_out[:, 0].reshape(width, bands),
-            part_out[:, 1].reshape(width, bands),
-        ],
-        1,
-    )
-    total = nd * slots * nj
-    if total != width:
-        where = (sources[:, None] * (slots * nj) + jnp.arange(slots * nj)[None]).reshape(-1)
-        parts = jnp.zeros((total, 2 * bands), f32).at[where].set(parts)
-        part_over = jnp.zeros((total, total), f32).at[where[:, None], where[None, :]].set(part_over)
-    summed = lax.psum(jnp.concatenate([parts, part_over], 1), "domain")
-    acted, plain, over = (
-        summed[:, :bands],
-        summed[:, bands : 2 * bands],
-        summed[:, 2 * bands :],
-    )
     slot = jnp.arange(slots, dtype=jnp.int32)
     live = (slot[None, :] < atom_count[:, None]).reshape(-1)
-    strength = jnp.where(live[:, None], coupling_all, 0.0).reshape(-1, 1)
-    weight_0 = strength * plain
-    plain_1 = SCALE_1 * (
-        acted + jnp.dot(over, weight_0, precision=lax.Precision.HIGHEST) - MIDDLE * plain
-    )
-    coef_p = SCALE_2 * (strength * plain_1 - (MIDDLE * SCALE_1) * weight_0)
-    coef_q = (SCALE_2 * SCALE_1) * weight_0
-    coef = jnp.stack(
-        [coef_q.reshape(nd, slots, nj, bands), coef_p.reshape(nd, slots, nj, bands)], 2
-    )
-    coef = coef[sources].reshape(count, bands).T
-
+    strength = jnp.where(live[:, None], coupling_all, 0.0)
+    highest = lax.Precision.HIGHEST
+    if count == nd * slots * 2 * nj:
+        summed = lax.psum(jnp.concatenate([part_out, part_over], 1), "domain")
+        both, over = summed[:, :bands], summed[:, bands:]
+        strength = jnp.concatenate([jnp.zeros_like(strength), strength], 1).reshape(-1, 1)
+        weight_0 = strength * both
+        plain_1 = SCALE_1 * (
+            jnp.roll(both, nj, 0) + jnp.dot(over, weight_0, precision=highest) - MIDDLE * both
+        )
+        coef = SCALE_2 * (
+            strength * plain_1
+            - (MIDDLE * SCALE_1) * weight_0
+            + SCALE_1 * jnp.roll(weight_0, -nj, 0)
+        )
+    else:
+        width, total = atoms * nj, nd * slots * nj
+        out = part_out.reshape(atoms, 2, nj, bands)
+        over = part_over.reshape(atoms, 2, nj, atoms, 2, nj)[:, 1, :, :, 1, :].reshape(width, width)
+        both = jnp.concatenate([out[:, 0].reshape(width, bands), out[:, 1].reshape(width, bands)], 1)
+        where = (sources[:, None] * (slots * nj) + jnp.arange(slots * nj)[None]).reshape(-1)
+        both = jnp.zeros((total, 2 * bands), f32).at[where].set(both)
+        over = jnp.zeros((total, total), f32).at[where[:, None], where[None, :]].set(over)
+        both, over = lax.psum(both, "domain"), lax.psum(over, "domain")
+        acted, plain = both[:, :bands], both[:, bands:]
+        strength = strength.reshape(-1, 1)
+        weight_0 = strength * plain
+        plain_1 = SCALE_1 * (
+            acted + jnp.dot(over, weight_0, precision=highest) - MIDDLE * plain
+        )
+        coef_p = SCALE_2 * (strength * plain_1 - (MIDDLE * SCALE_1) * weight_0)
+        coef_q = (SCALE_2 * SCALE_1) * weight_0
+        coef = jnp.stack(
+            [coef_q.reshape(nd, slots, nj, bands), coef_p.reshape(nd, slots, nj, bands)], 2
+        )
+        coef = coef[sources].reshape(count, bands)
+    coef = jnp.concatenate([coef, coef], 1).T
+    coef = lax.dynamic_slice_in_dim(coef, pos * share, bands, 0)
+
+    smem = pl.BlockSpec(memory_space=pltpu.SMEM)
+    part_block = pl.BlockSpec((each, chunk, nz), lambda i: (0, i, 0))
+    came = [local[h][(nd - p) % nd].reshape(each, rows, nz) for p in range(nd) for h in range(halves)]
     filtered, shared = call(
-        functools.partial(expand_kernel, chunk),
+        functools.partial(expand_kernel, chunk, nd, halves),
         grid=(rows // chunk,),
         in_specs=[
+            smem,
             pl.BlockSpec((chunk, count, nz), lambda i: (i, 0, 0)),
             pl.BlockSpec((bands, count), lambda i: (0, 0)),
-            pl.BlockSpec((bands, chunk, nz), lambda i: (0, i, 0)),
-        ],
+        ]
+        + [part_block] * (nd * halves),
         out_specs=[
             pl.BlockSpec((bands, chunk, nz), lambda i: (0, i, 0)),
             pl.BlockSpec((chunk, bands, nz), lambda i: (i, 0, 0)),
@@ -308,19 +374,24 @@
             jax.ShapeDtypeStruct((bands, rows, nz), f32),
             jax.ShapeDtypeStruct((rows, bands, nz), f32),
         ],
-    )(pq, coef, local)
-
-    shared = lax.all_to_all(shared.reshape(nb, rows // nb, bands, nz), "band", 0, 0)
+    )(pos.reshape(1), pq, coef, *came)
+
+    band = lax.axis_index("band")
+    given = [block_of(shared, band + p, nb) for p in range(nb)]
+    given = [shifted(part, "band", p) if p else part for p, part in enumerate(given)]
     gram = call(
-        functools.partial(gram_kernel, chunk),
+        functools.partial(gram_kernel, chunk, nb),
         grid=(rows // nb // chunk,),
-        in_specs=[pl.BlockSpec((nb, chunk, bands, nz), lambda i: (0, i, 0, 0))],
+        in_specs=[smem] + [pl.BlockSpec((chunk, bands, nz), lambda i: (i, 0, 0))] * nb,
         out_specs=pl.BlockSpec((nb * bands, nb * bands), lambda i: (0, 0)),
         out_shape=jax.ShapeDtypeStruct((nb * bands, nb * bands), f32),
-    )(shared)
-    gram = lax.psum(gram, ("domain", "band"))
-    gram = lax.dynamic_slice_in_dim(gram, lax.axis_index("band") * bands, bands, 0)
-    return filtered.reshape(orbitals.shape), gram / (nx * plane)
+        scratch_shapes=[pltpu.VMEM((nb * bands, 2 * nz), f32)],
+    )(band.reshape(1), *given)
+    own = block_of(gram, band, nb)
+    for p in range(1, nb):
+        own = own + shifted(block_of(gram, band + p, nb), "band", p)
+    own = summed_over(own, "domain")
+    return filtered.reshape(orbitals.shape), own / (nx * plane)
 
 
 def solution(mesh):

time: 655 us -> 447 us (0.68)
  blocking collectives: 268 us -> 112 us
  local copies, waits for them, and re-layouts: 91 us -> 16.8 us
  starting transfers between devices: 10.6 us -> 31.2 us
    psum x2 -> x1, waiting for transfers between devices: 121 us -> 0.01 us  [per_device(): summed = lax.psum(jnp.concatenate([part_out, part_over], 1), 'domain')]
    ppermute x0 -> x21, waiting for transfers between devices: none -> 116 us  [shifted(): lax.ppermute(values, axis, [(i, (i + by) % count) for i in range(count)])]
    all_gather x1, blocking collectives: 98.7 us -> 12.6 us  [per_device(): pot_all = lax.all_gather(potential, 'domain', axis=0, tiled=True)]
    all_to_all x1 -> x0, blocking collectives: 55 us -> none  [per_device(): lax.all_to_all(shared.reshape(nb, rows // nb, bands, nz), 'band', 0, 0)]
    slice x2 -> x4, local copies, waits for them, and re-layouts: 51.7 us -> 1.82 us  [the longest x2 1.73 us: per_device(): jnp.roll(both, nj, 0) + jnp.dot(over, weight_0, precision=highest)]
    reshape x2 -> x0, local copies, waits for them, and re-layouts: 32.2 us -> none  [the longest x1 31.4 us: per_device(): part_over.reshape(atoms, 2, nj, atoms, 2, nj)[:, 1, :, :, 1, :]]
    ppermute x0 -> x21, starting transfers between devices: none -> 31.1 us  [shifted(): lax.ppermute(values, axis, [(i, (i + by) % count) for i in range(count)])]
    all_gather x1, blocking collectives: 94.8 us -> 80.1 us  [per_device(): cells_all = lax.all_gather(sphere_cells, 'domain', axis=0, tiled=False)]
  transfers between devices with their start and end apart: 4 -> 22, of which waited for: 2 -> 10; matrix products, arithmetic and copies ran while one was open for 15% -> 3% of each run, Pallas kernels for 11% -> 27%
where the time goes in v2:
time: 447 us; the launch traced here: 444 us
  Pallas kernels  144 us (32%)
  waiting for transfers between devices  116 us (26%)
  blocking collectives  112 us (25%)
  starting transfers between devices  31.2 us (7%)
  local copies, waits for them, and re-layouts  16.8 us (4%)
  between operations  14.4 us (3%)
  other arithmetic  7.25 us (2%)
    ppermute x21, waiting for transfers between devices, shifted(): lax.ppermute(values, axis, [(i, (i + by) % count) for i in range(count)])  116 us
    all_gather x1, blocking collectives, per_device(): cells_all = lax.all_gather(sphere_cells, 'domain', axis=0, tiled=False)  80.1 us
    pallas_call x2, Pallas kernels, per_device(): call(functools.partial(local_kernel, nd), grid=(each,), in_specs=[block]...  46.4 us
    pallas_call x1, Pallas kernels, per_device(): call(functools.partial(build_kernel, nx, ny, slab), grid=(atoms,), in_spe...  37 us
    pallas_call x1, Pallas kernels, per_device(): call(functools.partial(project_kernel, chunk), grid=(rows // chunk,), in_...  34.6 us
    ppermute x21, starting transfers between devices, shifted(): lax.ppermute(values, axis, [(i, (i + by) % count) for i in range(count)])  31.1 us
    pallas_call x1, Pallas kernels, per_device(): call(functools.partial(expand_kernel, chunk, nd, halves), grid=(rows // c...  20.9 us
    all_gather x1, blocking collectives, per_device(): pot_all = lax.all_gather(potential, 'domain', axis=0, tiled=True)  12.6 us
  transfers between devices with their start and end apart: 22, of which 10 were waited for; matrix products, arithmetic and copies ran while one was open for 3% of the time, Pallas kernels for 27%

profile of v2, /device:TPU:1, one launch (start us, length us, event | category | flops | bytes accessed | tf_op | source)
XLA Modules:
  0.0 444.3 jit_solution(14151716337825348820)
XLA Ops:
  7.3 3.5 constant_dynamic-slice_fusion.7
  10.8 4.2 collective-permute-start
  15.5 2.8 collective-permute-start.3
  18.8 80.1 %all-gather.2 = s32[4,12,128]{2,1,0:T(8,128)S(1)} all-gather(s32[1,12,128]{2,1,0:T(8,128)S(1)} %bitcast.40), channel_id=2, replica_groups=mesh['groups'=2,'domain'=4,'band'=4] {'domain'}, dimensions={0}, use_global_device_ids=true | all-gather | bytes 30720 | tf_op jit(solution)/shard_map/all_gather | solution.py:271
  99.5 0.7 and_select_fusion
  100.2 10.4 %all-gather.1 = f32[48,4,128]{2,1,0:T(4,128)S(1)} all-gather(f32[12,4,128]{2,1,0:T(4,128)S(1)} %copy-done.8), channel_id=3, replica_groups=mesh['groups'=2,'domain'=4,'band'=4] {'domain'}, dimensions={0}, use_global_device_ids=true | all-gather | bytes 122880 | tf_op jit(solution)/shard_map/all_gather | solution.py:270
  110.5 1.2 gather_fusion.1
  111.8 0.9 and_select_fusion.1
  112.7 37.0 %shard_map.77.pq_ref = f32[128,384,128]{2,1,0:T(8,128)} custom-call(s32[48,1,128]{2,1,0:T(1,128)} %get-tuple-element.44.x_ref, s32[48,1,128]{2,1,0:T(1,128)} %get-tuple-element.43.y_ref, s32[48,1,128]{2,1,0:T(1,128)} %get-tuple-element.26.z_ref, f32[48,4,128]{2,1,0:T(4,128)} %bitcast.38, f32[128,128]{1,0:T(8,128)} %bitcast.39), custom_call_target="tpu_custom_call" | custom-call | flops 28800000000 | bytes 25165824 | tf_op jit(solution)/shard_map/pallas_call | solution.py:283
  149.7 34.6 %shard_map.78 = (f32[384,64]{1,0:T(8,128)}, f32[384,384]{1,0:T(8,128)}) custom-call(f32[128,384,128]{2,1,0:T(8,128)} %shard_map.77.pq_ref, f32[64,128,128]{2,1,0:T(8,128)} %bitcast.26), custom_call_target="tpu_custom_call" | custom-call | flops 22548578304 | bytes 25165824 | tf_op jit(solution)/shard_map/pallas_call | solution.py:299
  184.4 1.3 copy.23
  185.7 1.0 copy.22
  186.7 0.9 pad_maximum_fusion
  187.7 9.3 %all-gather.3 = f32[4,12,4]{1,2,0:T(4,128)S(1)} all-gather(f32[1,12,4]{1,2,0:T(4,128)S(1)} %bitcast.41), channel_id=1, replica_groups=mesh['groups'=2,'domain'=4,'band'=4] {'domain'}, dimensions={0}, use_global_device_ids=true | all-gather | bytes 960 | tf_op jit(solution)/shard_map/all_gather | solution.py:272
  197.5 12.6 %all_gather.23 = f32[32,16,128]{2,1,0:T(8,128)S(1)} all-gather(f32[8,16,128]{2,1,0:T(8,128)S(1)} %copy-done.7), channel_id=1, replica_groups=mesh['groups'=2,'domain'=4,'band'=4] {'domain'}, dimensions={0}, use_global_device_ids=true | all-gather | bytes 327680 | tf_op jit(solution)/shard_map/all_gather | solution.py:235
  210.2 0.7 select_select_fusion.refs_5_
  210.8 0.8 fusion.6.refs_4_
  211.6 23.2 %shard_map.79 = (f32[8,8,16,128]{3,2,1,0:T(8,128)}, f32[8,8,16,128]{3,2,1,0:T(8,128)}, f32[8,8,16,128]{3,2,1,0:T(8,128)}, f32[8,8,16,128]{3,2,1,0:T(8,128)}) custom-call(f32[8,8,16,128]{3,2,1,0:T(8,128)} %get-tuple-element.38.refs_0_, f32[8,8,16,128]{3,2,1,0:T(8,128)} %collective-permute-done.refs_1_, f32[8,8,16,128]{3,2,1,0:T(8,128)} %collective-permute-done.1.refs_2_, ...), custom_call_target="tpu_custom_call" | custom-call | flops 6291456000 | bytes 4194304 | tf_op jit(solution)/shard_map/pallas_call | solution.py:251
  234.8 3.3 collective-permute-start.6
  238.1 0.8 copy-done.11
  238.9 23.2 %shard_map.80 = (f32[8,8,16,128]{3,2,1,0:T(8,128)}, f32[8,8,16,128]{3,2,1,0:T(8,128)}, f32[8,8,16,128]{3,2,1,0:T(8,128)}, f32[8,8,16,128]{3,2,1,0:T(8,128)}) custom-call(f32[8,8,16,128]{3,2,1,0:T(8,128)} %get-tuple-element.34.refs_0_, f32[8,8,16,128]{3,2,1,0:T(8,128)} %collective-permute-done.3.refs_1_, f32[8,8,16,128]{3,2,1,0:T(8,128)} %collective-permute-done.4.refs_2_, ...), custom_call_target="tpu_custom_call" | custom-call | flops 6291456000 | bytes 4194304 | tf_op jit(solution)/shard_map/pallas_call | solution.py:251
  262.2 2.4 collective-permute-start.9
  264.6 1.4 collective-permute-start.10
  266.0 1.0 slice_multiply_fusion
  267.1 0.9 slice.35
  268.0 0.8 slice.34
  268.8 1.6 fusion.4
  270.4 0.7 fusion.8.coef_ref
  271.4 52.0 %collective-permute-done.8 = f32[8,8,16,128]{3,2,1,0:T(8,128)S(1)} collective-permute-done((f32[8,8,16,128]{3,2,1,0:T(8,128)}, f32[8,8,16,128]{3,2,1,0:T(8,128)S(1)}, u32[]{:S(2)}, u32[]{:S(2)}) %collective-permute-start.8) | collective-permute-done | bytes 524320 | tf_op jit(solution)/shard_map/ppermute | solution.py:196
  323.4 11.5 %collective-permute-done.9 = f32[8,8,16,128]{3,2,1,0:T(8,128)S(1)} collective-permute-done((f32[8,8,16,128]{3,2,1,0:T(8,128)}, f32[8,8,16,128]{3,2,1,0:T(8,128)S(1)}, u32[]{:S(2)}, u32[]{:S(2)}) %collective-permute-start.9) | collective-permute-done | bytes 524320 | tf_op jit(solution)/shard_map/ppermute | solution.py:196
  335.0 0.7 copy-done.4
  336.1 20.9 %shard_map.81 = (f32[64,128,128]{2,1,0:T(8,128)}, f32[128,64,128]{2,1,0:T(8,128)}) custom-call(s32[1]{0:T(128)} %bitcast.pos_ref, f32[128,384,128]{2,1,0:T(8,128)} %shard_map.77.pq_ref, f32[64,384]{1,0:T(8,128)} %fusion.8.coef_ref, f32[8,128,128]{2,1,0:T(8,128)} %bitcast.27, f32[8,128,128]{2,1,0:T(8,128)} %bitcast.29, f32[8,128,128]{2,1,0:T(8,128)} %bitcast.28, ...), custom_call_target="tpu_custom_call" | custom-call | tf_op jit(solution)/shard_map/pallas_call | solution.py:360
  357.1 4.0 constant_dynamic-slice_fusion.3
  361.1 8.3 %collective-permute-start.12 = (f32[32,64,128]{2,1,0:T(8,128)}, f32[32,64,128]{2,1,0:T(8,128)S(1)}, u32[]{:S(2)}, u32[]{:S(2)}) collective-permute-start(f32[32,64,128]{2,1,0:T(8,128)} %get-tuple-element.30), channel_id=1, source_target_pairs={{0,1},{1,2},{2,3},{3,0},{4,5},{5,6},{6,7},{7,4},{8,9},{9,10},{10,1... | collective-permute-start | bytes 3145736 | tf_op jit(solution)/shard_map/ppermute | solution.py:196
  369.8 22.6 %collective-permute-done.12.refs_1_ = f32[32,64,128]{2,1,0:T(8,128)S(1)} collective-permute-done((f32[32,64,128]{2,1,0:T(8,128)}, f32[32,64,128]{2,1,0:T(8,128)S(1)}, u32[]{:S(2)}, u32[]{:S(2)}) %collective-permute-start.12) | collective-permute-done | bytes 1048608 | tf_op jit(solution)/shard_map/ppermute | solution.py:196
  392.3 23.1 %collective-permute-done.13.refs_2_ = f32[32,64,128]{2,1,0:T(8,128)} collective-permute-done((f32[32,64,128]{2,1,0:T(8,128)S(1)}, f32[32,64,128]{2,1,0:T(8,128)}, u32[]{:S(2)}, u32[]{:S(2)}) %collective-permute-start.13) | collective-permute-done | bytes 1048608 | tf_op jit(solution)/shard_map/ppermute | solution.py:196
  415.7 5.6 %shard_map.82 = f32[256,256]{1,0:T(8,128)} custom-call(s32[1]{0:T(128)} %bitcast.21.pos_ref, f32[32,64,128]{2,1,0:T(8,128)} %get-tuple-element.31.refs_0_, f32[32,64,128]{2,1,0:T(8,128)} %copy-done, f32[32,64,128]{2,1,0:T(8,128)} %collective-permute-done.13.refs_2_, f32[32,64,128]{2,1,0:T(8,128)} %collective-permute-done.14.refs_3_), custom_call_target="tpu_custom_call" | custom-call | tf_op jit(solution)/shard_map/pallas_call | solution.py:382
  421.3 0.9 constant_dynamic-slice_fusion.2
  422.2 1.4 collective-permute-start.16
  423.6 0.7 collective-permute-start.17
  424.3 2.1 collective-permute-done.16
  426.5 0.8 collective-permute-done.17
  427.3 0.9 add_add_fusion
  428.2 0.9 collective-permute-start.18
  429.1 1.9 collective-permute-start.19
  431.0 2.3 collective-permute-start.20
  433.8 3.0 collective-permute-done.19
  436.8 0.6 add_multiply_fusion
  (66 shorter events, 4.5 us)
Async XLA Ops:
  7.2 258.9 %all-reduce.3.cloned.1.call-start = ((), (), s32[]{:S(2)}) async-start(), calls=%async_computation | async-start | bytes 1376256 | tf_op jit(solution)/shard_map/psum | solution.py:321
  7.3 11.5 %copy-start.9 = (s32[12,128]{1,0:T(8,128)S(1)}, s32[12,128]{1,0:T(8,128)}, u32[]{:S(2)}) copy-start(s32[12,128]{1,0:T(8,128)} %param.10) | copy-start | bytes 18436
  7.3 92.8 %copy-start.8 = (f32[12,4,128]{2,1,0:T(4,128)S(1)}, f32[12,4,128]{2,1,0:T(4,128)}, u32[]{:S(2)}) copy-start(f32[12,4,128]{2,1,0:T(4,128)} %param.8) | copy-start | bytes 73732
  10.8 200.8 %collective-permute-start = (f32[8,8,16,128]{3,2,1,0:T(8,128)}, f32[8,8,16,128]{3,2,1,0:T(8,128)}, u32[]{:S(2)}, u32[]{:S(2)}) collective-permute-start(f32[8,8,16,128]{3,2,1,0:T(8,128)} %get-tuple-element.37), channel_id=1, source_target_pairs={{0,12},{4,0},{8,4},{12,8},{1,13},{5,1},{9,5},{13,9},{2,14},{6,2},{... | collective-permute-start | bytes 1572872 | tf_op jit(solution)/shard_map/ppermute | solution.py:196
  15.0 196.6 %collective-permute-start.1 = (f32[8,8,16,128]{3,2,1,0:T(8,128)S(1)}, f32[8,8,16,128]{3,2,1,0:T(8,128)}, u32[]{:S(2)}, u32[]{:S(2)}) collective-permute-start(f32[8,8,16,128]{3,2,1,0:T(8,128)S(1)} %get-tuple-element.36), channel_id=1, source_target_pairs={{0,8},{4,12},{8,0},{12,4},{1,9},{5,13},{9,1},{13,5},{2,10},{6,14},... | collective-permute-start | bytes 1572872 | tf_op jit(solution)/shard_map/ppermute | solution.py:196
  15.0 196.6 %collective-permute-start.2 = (f32[8,8,16,128]{3,2,1,0:T(8,128)S(1)}, f32[8,8,16,128]{3,2,1,0:T(8,128)}, u32[]{:S(2)}, u32[]{:S(2)}) collective-permute-start(f32[8,8,16,128]{3,2,1,0:T(8,128)S(1)} %get-tuple-element.35), channel_id=1, source_target_pairs={{0,4},{4,8},{8,12},{12,0},{1,5},{5,9},{9,13},{13,1},{2,6},{6,10},{... | collective-permute-start | bytes 1572872 | tf_op jit(solution)/shard_map/ppermute | solution.py:196
  15.5 222.6 %collective-permute-start.3 = (f32[8,8,16,128]{3,2,1,0:T(8,128)S(1)}, f32[8,8,16,128]{3,2,1,0:T(8,128)}, u32[]{:S(2)}, u32[]{:S(2)}) collective-permute-start(f32[8,8,16,128]{3,2,1,0:T(8,128)S(1)} %get-tuple-element.33), channel_id=1, source_target_pairs={{0,12},{4,0},{8,4},{12,8},{1,13},{5,1},{9,5},{13,9},{2,14},{6,2},{... | collective-permute-start | bytes 1572872 | tf_op jit(solution)/shard_map/ppermute | solution.py:196
  18.3 219.8 %collective-permute-start.4 = (f32[8,8,16,128]{3,2,1,0:T(8,128)S(1)}, f32[8,8,16,128]{3,2,1,0:T(8,128)}, u32[]{:S(2)}, u32[]{:S(2)}) collective-permute-start(f32[8,8,16,128]{3,2,1,0:T(8,128)S(1)} %get-tuple-element.39), channel_id=1, source_target_pairs={{0,8},{4,12},{8,0},{12,4},{1,9},{5,13},{9,1},{13,5},{2,10},{6,14},... | collective-permute-start | bytes 1572872 | tf_op jit(solution)/shard_map/ppermute | solution.py:196
  149.7 38.0 %copy-start.10 = (f32[12,4]{0,1:T(4,128)S(1)}, f32[12,4]{0,1:T(4,128)}, u32[]{:S(2)}) copy-start(f32[12,4]{0,1:T(4,128)} %param.9) | copy-start | bytes 580
  149.7 47.4 %copy-start.12 = (s32[4]{0:T(128)S(1)}, s32[4]{0:T(128)}, u32[]{:S(2)}) copy-start(s32[4]{0:T(128)} %param.11) | copy-start | bytes 52
  149.7 47.8 %copy-start.7 = (f32[8,16,128]{2,1,0:T(8,128)S(1)}, f32[8,16,128]{2,1,0:T(8,128)}, u32[]{:S(2)}) copy-start(f32[8,16,128]{2,1,0:T(8,128)} %param.7) | copy-start | bytes 196612
  211.6 26.5 %collective-permute-start.5 = (f32[8,8,16,128]{3,2,1,0:T(8,128)S(1)}, f32[8,8,16,128]{3,2,1,0:T(8,128)S(1)}, u32[]{:S(2)}, u32[]{:S(2)}) collective-permute-start(f32[8,8,16,128]{3,2,1,0:T(8,128)S(1)} %get-tuple-element.32), channel_id=1, source_target_pairs={{0,4},{4,8},{8,12},{12,0},{1,5},{5,9},{9,13},{13,1},{2,6},{6,10},{... | collective-permute-start | bytes 1572872 | tf_op jit(solution)/shard_map/ppermute | solution.py:196
  234.8 31.1 %collective-permute-start.6 = (f32[8,8,16,128]{3,2,1,0:T(8,128)}, f32[8,8,16,128]{3,2,1,0:T(8,128)S(1)}, u32[]{:S(2)}, u32[]{:S(2)}) collective-permute-start(f32[8,8,16,128]{3,2,1,0:T(8,128)} %get-tuple-element.18), channel_id=1, source_target_pairs={{0,12},{4,0},{8,4},{12,8},{1,13},{5,1},{9,5},{13,9},{2,14},{6,2},{... | collective-permute-start | bytes 1572872 | tf_op jit(solution)/shard_map/ppermute | solution.py:196
  238.1 0.8 copy-start.11
  262.1 9.3 %collective-permute-start.7 = (f32[8,8,16,128]{3,2,1,0:T(8,128)}, f32[8,8,16,128]{3,2,1,0:T(8,128)S(1)}, u32[]{:S(2)}, u32[]{:S(2)}) collective-permute-start(f32[8,8,16,128]{3,2,1,0:T(8,128)} %get-tuple-element.19), channel_id=1, source_target_pairs={{0,12},{4,0},{8,4},{12,8},{1,13},{5,1},{9,5},{13,9},{2,14},{6,2},{... | collective-permute-start | bytes 1572872 | tf_op jit(solution)/shard_map/ppermute | solution.py:196
  262.1 61.3 %collective-permute-start.8 = (f32[8,8,16,128]{3,2,1,0:T(8,128)}, f32[8,8,16,128]{3,2,1,0:T(8,128)S(1)}, u32[]{:S(2)}, u32[]{:S(2)}) collective-permute-start(f32[8,8,16,128]{3,2,1,0:T(8,128)} %get-tuple-element.20), channel_id=1, source_target_pairs={{0,8},{4,12},{8,0},{12,4},{1,9},{5,13},{9,1},{13,5},{2,10},{6,14},... | collective-permute-start | bytes 1572872 | tf_op jit(solution)/shard_map/ppermute | solution.py:196
  262.2 72.7 %collective-permute-start.9 = (f32[8,8,16,128]{3,2,1,0:T(8,128)}, f32[8,8,16,128]{3,2,1,0:T(8,128)S(1)}, u32[]{:S(2)}, u32[]{:S(2)}) collective-permute-start(f32[8,8,16,128]{3,2,1,0:T(8,128)} %get-tuple-element.21), channel_id=1, source_target_pairs={{0,8},{4,12},{8,0},{12,4},{1,9},{5,13},{9,1},{13,5},{2,10},{6,14},... | collective-permute-start | bytes 1572872 | tf_op jit(solution)/shard_map/ppermute | solution.py:196
  264.6 70.4 %collective-permute-start.10 = (f32[8,8,16,128]{3,2,1,0:T(8,128)}, f32[8,8,16,128]{3,2,1,0:T(8,128)S(1)}, u32[]{:S(2)}, u32[]{:S(2)}) collective-permute-start(f32[8,8,16,128]{3,2,1,0:T(8,128)} %get-tuple-element.22), channel_id=1, source_target_pairs={{0,4},{4,8},{8,12},{12,0},{1,5},{5,9},{9,13},{13,1},{2,6},{6,10},{... | collective-permute-start | bytes 1572872 | tf_op jit(solution)/shard_map/ppermute | solution.py:196
  266.0 69.0 %copy-start.1 = (f32[8,8,16,128]{3,2,1,0:T(8,128)}, f32[8,8,16,128]{3,2,1,0:T(8,128)S(1)}, u32[]{:S(2)}) copy-start(f32[8,8,16,128]{3,2,1,0:T(8,128)S(1)} %collective-permute-done.6) | copy-start | bytes 1572868
  266.0 69.0 %collective-permute-start.11 = (f32[8,8,16,128]{3,2,1,0:T(8,128)}, f32[8,8,16,128]{3,2,1,0:T(8,128)S(1)}, u32[]{:S(2)}, u32[]{:S(2)}) collective-permute-start(f32[8,8,16,128]{3,2,1,0:T(8,128)} %get-tuple-element.23), channel_id=1, source_target_pairs={{0,4},{4,8},{8,12},{12,0},{1,5},{5,9},{9,13},{13,1},{2,6},{6,10},{... | collective-permute-start | bytes 1572872 | tf_op jit(solution)/shard_map/ppermute | solution.py:196
  271.4 63.6 %copy-start.2 = (f32[8,8,16,128]{3,2,1,0:T(8,128)}, f32[8,8,16,128]{3,2,1,0:T(8,128)S(1)}, u32[]{:S(2)}) copy-start(f32[8,8,16,128]{3,2,1,0:T(8,128)S(1)} %collective-permute-done.7) | copy-start | bytes 1572868
  323.4 11.6 %copy-start.3 = (f32[8,8,16,128]{3,2,1,0:T(8,128)}, f32[8,8,16,128]{3,2,1,0:T(8,128)S(1)}, u32[]{:S(2)}) copy-start(f32[8,8,16,128]{3,2,1,0:T(8,128)S(1)} %collective-permute-done.8) | copy-start | bytes 1572868
  334.9 0.8 copy-start.4
  334.9 1.0 copy-start.5
  334.9 1.2 copy-start.6
  361.1 31.3 %collective-permute-start.12 = (f32[32,64,128]{2,1,0:T(8,128)}, f32[32,64,128]{2,1,0:T(8,128)S(1)}, u32[]{:S(2)}, u32[]{:S(2)}) collective-permute-start(f32[32,64,128]{2,1,0:T(8,128)} %get-tuple-element.30), channel_id=1, source_target_pairs={{0,1},{1,2},{2,3},{3,0},{4,5},{5,6},{6,7},{7,4},{8,9},{9,10},{10,1... | collective-permute-start | bytes 3145736 | tf_op jit(solution)/shard_map/ppermute | solution.py:196
  369.4 46.0 %collective-permute-start.13 = (f32[32,64,128]{2,1,0:T(8,128)S(1)}, f32[32,64,128]{2,1,0:T(8,128)}, u32[]{:S(2)}, u32[]{:S(2)}) collective-permute-start(f32[32,64,128]{2,1,0:T(8,128)S(1)} %get-tuple-element.29), channel_id=1, source_target_pairs={{0,2},{1,3},{2,0},{3,1},{4,6},{5,7},{6,4},{7,5},{8,10},{9,11},{10,... | collective-permute-start | bytes 3145736 | tf_op jit(solution)/shard_map/ppermute | solution.py:196
  369.5 46.2 %collective-permute-start.14 = (f32[32,64,128]{2,1,0:T(8,128)S(1)}, f32[32,64,128]{2,1,0:T(8,128)}, u32[]{:S(2)}, u32[]{:S(2)}) collective-permute-start(f32[32,64,128]{2,1,0:T(8,128)S(1)} %get-tuple-element.28), channel_id=1, source_target_pairs={{0,3},{1,0},{2,1},{3,2},{4,7},{5,4},{6,5},{7,6},{8,11},{9,8},{10,9... | collective-permute-start | bytes 3145736 | tf_op jit(solution)/shard_map/ppermute | solution.py:196
  392.3 23.4 %copy-start = (f32[32,64,128]{2,1,0:T(8,128)}, f32[32,64,128]{2,1,0:T(8,128)S(1)}, u32[]{:S(2)}) copy-start(f32[32,64,128]{2,1,0:T(8,128)S(1)} %collective-permute-done.12.refs_1_) | copy-start | bytes 3145732
  422.2 2.2 collective-permute-start.15
  422.2 4.2 collective-permute-start.16
  423.6 3.7 collective-permute-start.17
  428.2 5.7 %collective-permute-start.18 = (f32[64,256]{1,0:T(8,128)S(1)}, f32[64,256]{1,0:T(8,128)S(1)}, u32[]{:S(2)}, u32[]{:S(2)}) collective-permute-start(f32[64,256]{1,0:T(8,128)S(1)} %add_add_fusion), channel_id=1, source_target_pairs={{0,4},{4,8},{8,12},{12,0},{1,5},{5,9},{9,13},{13,1},{2,6},{6,10},{... | collective-permute-start | bytes 196616 | tf_op jit(solution)/shard_map/ppermute | solution.py:196
  429.1 7.7 %collective-permute-start.19 = (f32[64,256]{1,0:T(8,128)S(1)}, f32[64,256]{1,0:T(8,128)S(1)}, u32[]{:S(2)}, u32[]{:S(2)}) collective-permute-start(f32[64,256]{1,0:T(8,128)S(1)} %add_add_fusion), channel_id=1, source_target_pairs={{0,8},{4,12},{8,0},{12,4},{1,9},{5,13},{9,1},{13,5},{2,10},{6,14},... | collective-permute-start | bytes 196616 | tf_op jit(solution)/shard_map/ppermute | solution.py:196
  431.0 5.8 %collective-permute-start.20 = (f32[64,256]{1,0:T(8,128)S(1)}, f32[64,256]{1,0:T(8,128)S(1)}, u32[]{:S(2)}, u32[]{:S(2)}) collective-permute-start(f32[64,256]{1,0:T(8,128)S(1)} %add_add_fusion), channel_id=1, source_target_pairs={{0,12},{4,0},{8,4},{12,8},{1,13},{5,1},{9,5},{13,9},{2,14},{6,2},{... | collective-permute-start | bytes 196616 | tf_op jit(solution)/shard_map/ppermute | solution.py:196
Sparse Core Ops, SparseCore 0:
  187.8 50.3 all-reduce.2

commit v3 on v2

--- a/solution.py
+++ b/solution.py
@@ -232,7 +232,23 @@
     halves = 2 if share % 2 == 0 else 1
     each = share // halves
 
-    pot_all = lax.all_gather(potential, "domain", axis=0, tiled=True)
+    packed = jnp.concatenate(
+        [
+            projector.reshape(slots * nj, sph),
+            sphere_cells.astype(f32),
+            jnp.pad(coupling, ((0, 0), (0, sph - nj))),
+            potential.reshape(rows, nz),
+        ],
+        0,
+    )
+    packed = lax.all_gather(packed, "domain", axis=0, tiled=False)
+    orbitals_later, packed = lax.optimization_barrier((orbitals, packed))
+    ends = (slots * nj, slots * nj + slots, slots * nj + 2 * slots)
+    proj_all = packed[:, : ends[0]].reshape(nd, slots, nj, sph)
+    cells_all = packed[:, ends[0] : ends[1]].astype(jnp.int32)
+    coupling_all = packed[:, ends[1] : ends[2], :nj].reshape(nd * slots, nj)
+    pot_all = packed[:, ends[2] :].reshape(nx, ny, nz)
+
     pot_all = lax.dynamic_slice_in_dim(
         jnp.concatenate([pot_all, pot_all], 0), pos * slab, nx, 0
     )
@@ -242,7 +258,7 @@
 
     def sent(h, p):
         start = (pos - p) % nd * share + h * each
-        part = lax.dynamic_slice_in_dim(orbitals, start, each, 0)
+        part = lax.dynamic_slice_in_dim(orbitals_later, start, each, 0)
         return shifted(part, "domain", -p) if p else part
 
     local = []
@@ -267,9 +283,6 @@
         local.append([shifted(part, "domain", p) if p else part for p, part in enumerate(results)])
 
     near = -(-(REACH + HALO) // slab)
-    proj_all = lax.all_gather(projector, "domain", axis=0, tiled=False)
-    cells_all = lax.all_gather(sphere_cells, "domain", axis=0, tiled=False)
-    coupling_all = lax.all_gather(coupling, "domain", axis=0, tiled=True)
     if nd <= 2 * near + 1:
         sources = jnp.arange(nd, dtype=jnp.int32)
     else:

time: 447 us -> 350 us (0.78)
  blocking collectives: 112 us -> 14 us
    all_gather x4 -> x1, blocking collectives: 112 us -> 14 us  [per_device(): packed = lax.all_gather(packed, 'domain', axis=0, tiled=False)]
  transfers between devices with their start and end apart: 22 -> 22, of which waited for: 10 -> 10; matrix products, arithmetic and copies ran while one was open for 3% -> 4% of each run, Pallas kernels for 27% -> 34%
where the time goes in v3:
time: 350 us; the launch traced here: 346 us
  Pallas kernels  144 us (41%)
  waiting for transfers between devices  117 us (33%)
  starting transfers between devices  27.6 us (8%)
  local copies, waits for them, and re-layouts  18.2 us (5%)
  between operations  14.4 us (4%)
  blocking collectives  14 us (4%)
  other arithmetic  8.82 us (3%)
    ppermute x21, waiting for transfers between devices, shifted(): lax.ppermute(values, axis, [(i, (i + by) % count) for i in range(count)])  117 us
    pallas_call x2, Pallas kernels, per_device(): call(functools.partial(local_kernel, nd), grid=(each,), in_specs=[block]...  46.3 us
    pallas_call x1, Pallas kernels, per_device(): call(functools.partial(build_kernel, nx, ny, slab), grid=(atoms,), in_spe...  37 us
    pallas_call x1, Pallas kernels, per_device(): call(functools.partial(project_kernel, chunk), grid=(rows // chunk,), in_...  34.6 us
    ppermute x21, starting transfers between devices, shifted(): lax.ppermute(values, axis, [(i, (i + by) % count) for i in range(count)])  27.6 us
    pallas_call x1, Pallas kernels, per_device(): call(functools.partial(expand_kernel, chunk, nd, halves), grid=(rows // c...  20.9 us
    all_gather x1, blocking collectives, per_device(): packed = lax.all_gather(packed, 'domain', axis=0, tiled=False)  14 us
  transfers between devices with their start and end apart: 22, of which 10 were waited for; matrix products, arithmetic and copies ran while one was open for 4% of the time, Pallas kernels for 34%

profile of v3, /device:TPU:1, one launch (start us, length us, event | category | flops | bytes accessed | tf_op | source)
XLA Modules:
  0.0 345.9 jit_solution(2140357358791801480)
XLA Ops:
  7.3 0.7 convert_element_type.8
  8.0 0.8 copy.11
  8.8 0.8 fusion.7
  9.6 14.0 %all-gather = f32[800,128]{1,0:T(8,128)S(1)} all-gather(f32[200,128]{1,0:T(8,128)S(1)} %fusion.7), channel_id=2, replica_groups=mesh['groups'=2,'domain'=4,'band'=4] {'domain'}, dimensions={0}, use_global_device_ids=true | all-gather | bytes 512000 | tf_op jit(solution)/shard_map/all_gather | solution.py:244
  23.6 3.8 %constant_dynamic-slice_fusion.7 = (f32[8,8,16,128]{3,2,1,0:T(8,128)S(1)}, f32[8,8,16,128]{3,2,1,0:T(8,128)S(1)}, f32[8,8,16,128]{3,2,1,0:T(8,128)S(1)}, f32[8,8...) fusion(f32[64,8,16,128]{3,2,1,0:T(8,128)} %param.6, ...), kind=kLoop, calls=%fused_computation.60 | loop fusion | bytes 8388640 | tf_op jit(solution)/shard_map/dynamic_slice | solution.py:261
  27.4 1.9 collective-permute-start
  29.6 3.0 collective-permute-start.3
  33.8 0.7 and_select_fusion
  34.5 1.2 gather_fusion.1
  35.7 0.9 and_select_fusion.1
  36.6 37.0 %shard_map.77.pq_ref = f32[128,384,128]{2,1,0:T(8,128)} custom-call(s32[48,1,128]{2,1,0:T(1,128)} %get-tuple-element.48.x_ref, s32[48,1,128]{2,1,0:T(1,128)} %get-tuple-element.47.y_ref, s32[48,1,128]{2,1,0:T(1,128)} %get-tuple-element.30.z_ref, f32[48,4,128]{2,1,0:T(4,128)} %bitcast.44, f32[128,128]{1,0:T(8,128)} %bitcast.46), custom_call_target="tpu_custom_call" | custom-call | flops 28800000000 | bytes 25165824 | tf_op jit(solution)/shard_map/pallas_call | solution.py:296
  73.6 34.6 %shard_map.78 = (f32[384,64]{1,0:T(8,128)}, f32[384,384]{1,0:T(8,128)}) custom-call(f32[128,384,128]{2,1,0:T(8,128)} %shard_map.77.pq_ref, f32[64,128,128]{2,1,0:T(8,128)} %bitcast.27), custom_call_target="tpu_custom_call" | custom-call | flops 22548578304 | bytes 25165824 | tf_op jit(solution)/shard_map/pallas_call | solution.py:312
  108.2 1.3 copy.17
  109.5 1.0 copy.16
  110.6 0.9 pad_maximum_fusion
  112.4 0.7 select_select_fusion.refs_5_
  113.1 0.8 fusion.6.refs_4_
  113.9 23.2 %shard_map.79 = (f32[8,8,16,128]{3,2,1,0:T(8,128)}, f32[8,8,16,128]{3,2,1,0:T(8,128)}, f32[8,8,16,128]{3,2,1,0:T(8,128)}, f32[8,8,16,128]{3,2,1,0:T(8,128)}) custom-call(f32[8,8,16,128]{3,2,1,0:T(8,128)} %get-tuple-element.43.refs_0_, f32[8,8,16,128]{3,2,1,0:T(8,128)} %collective-permute-done.refs_1_, f32[8,8,16,128]{3,2,1,0:T(8,128)} %collective-permute-done.1.refs_2_, ...), custom_call_target="tpu_custom_call" | custom-call | flops 6291456000 | bytes 4194304 | tf_op jit(solution)/shard_map/pallas_call | solution.py:267
  137.1 3.3 collective-permute-start.6
  140.4 0.8 copy-done.7
  141.2 23.2 %shard_map.80 = (f32[8,8,16,128]{3,2,1,0:T(8,128)}, f32[8,8,16,128]{3,2,1,0:T(8,128)}, f32[8,8,16,128]{3,2,1,0:T(8,128)}, f32[8,8,16,128]{3,2,1,0:T(8,128)}) custom-call(f32[8,8,16,128]{3,2,1,0:T(8,128)} %get-tuple-element.39.refs_0_, f32[8,8,16,128]{3,2,1,0:T(8,128)} %collective-permute-done.3.refs_1_, f32[8,8,16,128]{3,2,1,0:T(8,128)} %collective-permute-done.4.refs_2_, ...), custom_call_target="tpu_custom_call" | custom-call | flops 6291456000 | bytes 4194304 | tf_op jit(solution)/shard_map/pallas_call | solution.py:267
  164.5 2.4 collective-permute-start.9
  166.8 1.4 collective-permute-start.10
  168.3 1.0 slice_multiply_fusion
  169.4 0.9 slice.51
  170.3 0.8 slice.50
  171.1 1.6 fusion.4
  172.7 0.7 fusion.10.coef_ref
  173.6 53.2 %collective-permute-done.8 = f32[8,8,16,128]{3,2,1,0:T(8,128)S(1)} collective-permute-done((f32[8,8,16,128]{3,2,1,0:T(8,128)}, f32[8,8,16,128]{3,2,1,0:T(8,128)S(1)}, u32[]{:S(2)}, u32[]{:S(2)}) %collective-permute-start.8) | collective-permute-done | bytes 524320 | tf_op jit(solution)/shard_map/ppermute | solution.py:196
  226.8 11.5 %collective-permute-done.9 = f32[8,8,16,128]{3,2,1,0:T(8,128)S(1)} collective-permute-done((f32[8,8,16,128]{3,2,1,0:T(8,128)}, f32[8,8,16,128]{3,2,1,0:T(8,128)S(1)}, u32[]{:S(2)}, u32[]{:S(2)}) %collective-permute-start.9) | collective-permute-done | bytes 524320 | tf_op jit(solution)/shard_map/ppermute | solution.py:196
  238.3 0.7 copy-done.4
  239.5 20.9 %shard_map.81 = (f32[64,128,128]{2,1,0:T(8,128)}, f32[128,64,128]{2,1,0:T(8,128)}) custom-call(s32[1]{0:T(128)} %bitcast.pos_ref, f32[128,384,128]{2,1,0:T(8,128)} %shard_map.77.pq_ref, f32[64,384]{1,0:T(8,128)} %fusion.10.coef_ref, f32[8,128,128]{2,1,0:T(8,128)} %bitcast.33, f32[8,128,128]{2,1,0:T(8,128)} %bitcast.35, f32[8,128,128]{2,1,0:T(8,128)} %bitcast.34, ...), custom_call_target="tpu_custom_call" | custom-call | tf_op jit(solution)/shard_map/pallas_call | solution.py:373
  260.4 4.0 %constant_dynamic-slice_fusion.3 = (f32[32,64,128]{2,1,0:T(8,128)S(1)}, f32[32,64,128]{2,1,0:T(8,128)S(1)}, f32[32,64,128]{2,1,0:T(8,128)}, f32[32,64,128]{2,1,0:T(8,128)}) fusion(f32[128,64,128]{2,1,0:T(8,128)} %get-tuple-element.29, s32[]{:T(128)S(6)} %select_n.220, s32[]{:T(128)S(6)} %select_n.218, s32[]{:T(128)S(6)} %select_n.216, s32[]{:T(128)S(6)} %select_n.214), kind=kLoop, calls=%fused_computation.56 | loop fusion | bytes 8388624 | tf_op jit(solution)/shard_map/dynamic_slice | solution.py:211
  264.4 7.7 %collective-permute-start.12 = (f32[32,64,128]{2,1,0:T(8,128)}, f32[32,64,128]{2,1,0:T(8,128)S(1)}, u32[]{:S(2)}, u32[]{:S(2)}) collective-permute-start(f32[32,64,128]{2,1,0:T(8,128)} %get-tuple-element.34), channel_id=1, source_target_pairs={{0,1},{1,2},{2,3},{3,0},{4,5},{5,6},{6,7},{7,4},{8,9},{9,10},{10,1... | collective-permute-start | bytes 3145736 | tf_op jit(solution)/shard_map/ppermute | solution.py:196
  272.6 22.6 %collective-permute-done.12.refs_1_ = f32[32,64,128]{2,1,0:T(8,128)S(1)} collective-permute-done((f32[32,64,128]{2,1,0:T(8,128)}, f32[32,64,128]{2,1,0:T(8,128)S(1)}, u32[]{:S(2)}, u32[]{:S(2)}) %collective-permute-start.12) | collective-permute-done | bytes 1048608 | tf_op jit(solution)/shard_map/ppermute | solution.py:196
  295.1 23.2 %collective-permute-done.13.refs_2_ = f32[32,64,128]{2,1,0:T(8,128)} collective-permute-done((f32[32,64,128]{2,1,0:T(8,128)S(1)}, f32[32,64,128]{2,1,0:T(8,128)}, u32[]{:S(2)}, u32[]{:S(2)}) %collective-permute-start.13) | collective-permute-done | bytes 1048608 | tf_op jit(solution)/shard_map/ppermute | solution.py:196
  318.6 5.6 %shard_map.82 = f32[256,256]{1,0:T(8,128)} custom-call(s32[1]{0:T(128)} %bitcast.22.pos_ref, f32[32,64,128]{2,1,0:T(8,128)} %get-tuple-element.35.refs_0_, f32[32,64,128]{2,1,0:T(8,128)} %copy-done, f32[32,64,128]{2,1,0:T(8,128)} %collective-permute-done.13.refs_2_, f32[32,64,128]{2,1,0:T(8,128)} %collective-permute-done.14.refs_3_), custom_call_target="tpu_custom_call" | custom-call | tf_op jit(solution)/shard_map/pallas_call | solution.py:395
  324.2 0.9 constant_dynamic-slice_fusion.2
  325.1 1.3 collective-permute-start.16
  326.4 0.7 collective-permute-start.17
  327.1 2.0 collective-permute-done.16
  329.1 1.0 collective-permute-done.17
  330.1 0.9 add_add_fusion
  331.2 1.9 collective-permute-start.19
  333.1 2.3 collective-permute-start.20
  335.4 1.1 collective-permute-done.18
  336.6 1.9 collective-permute-done.20
  338.4 0.6 add_multiply_fusion
  (62 shorter events, 4.4 us)
Async XLA Ops:
  7.2 161.1 %all-reduce.4.cloned.1.call-start = ((), (), s32[]{:S(2)}) async-start(), calls=%async_computation | async-start | bytes 1376256 | tf_op jit(solution)/shard_map/psum | solution.py:334
  27.4 86.5 %collective-permute-start = (f32[8,8,16,128]{3,2,1,0:T(8,128)}, f32[8,8,16,128]{3,2,1,0:T(8,128)}, u32[]{:S(2)}, u32[]{:S(2)}) collective-permute-start(f32[8,8,16,128]{3,2,1,0:T(8,128)} %get-tuple-element.42), channel_id=1, source_target_pairs={{0,12},{4,0},{8,4},{12,8},{1,13},{5,1},{9,5},{13,9},{2,14},{6,2},{... | collective-permute-start | bytes 1572872 | tf_op jit(solution)/shard_map/ppermute | solution.py:196
  29.3 84.6 %collective-permute-start.1 = (f32[8,8,16,128]{3,2,1,0:T(8,128)}, f32[8,8,16,128]{3,2,1,0:T(8,128)}, u32[]{:S(2)}, u32[]{:S(2)}) collective-permute-start(f32[8,8,16,128]{3,2,1,0:T(8,128)} %get-tuple-element.41), channel_id=1, source_target_pairs={{0,8},{4,12},{8,0},{12,4},{1,9},{5,13},{9,1},{13,5},{2,10},{6,14},... | collective-permute-start | bytes 1572872 | tf_op jit(solution)/shard_map/ppermute | solution.py:196
  29.3 84.6 %collective-permute-start.2 = (f32[8,8,16,128]{3,2,1,0:T(8,128)S(1)}, f32[8,8,16,128]{3,2,1,0:T(8,128)}, u32[]{:S(2)}, u32[]{:S(2)}) collective-permute-start(f32[8,8,16,128]{3,2,1,0:T(8,128)S(1)} %get-tuple-element.40), channel_id=1, source_target_pairs={{0,4},{4,8},{8,12},{12,0},{1,5},{5,9},{9,13},{13,1},{2,6},{6,10},{... | collective-permute-start | bytes 1572872 | tf_op jit(solution)/shard_map/ppermute | solution.py:196
  29.6 110.8 %collective-permute-start.3 = (f32[8,8,16,128]{3,2,1,0:T(8,128)S(1)}, f32[8,8,16,128]{3,2,1,0:T(8,128)}, u32[]{:S(2)}, u32[]{:S(2)}) collective-permute-start(f32[8,8,16,128]{3,2,1,0:T(8,128)S(1)} %get-tuple-element.38), channel_id=1, source_target_pairs={{0,12},{4,0},{8,4},{12,8},{1,13},{5,1},{9,5},{13,9},{2,14},{6,2},{... | collective-permute-start | bytes 1572872 | tf_op jit(solution)/shard_map/ppermute | solution.py:196
  32.6 107.8 %collective-permute-start.4 = (f32[8,8,16,128]{3,2,1,0:T(8,128)S(1)}, f32[8,8,16,128]{3,2,1,0:T(8,128)}, u32[]{:S(2)}, u32[]{:S(2)}) collective-permute-start(f32[8,8,16,128]{3,2,1,0:T(8,128)S(1)} %get-tuple-element.37), channel_id=1, source_target_pairs={{0,8},{4,12},{8,0},{12,4},{1,9},{5,13},{9,1},{13,5},{2,10},{6,14},... | collective-permute-start | bytes 1572872 | tf_op jit(solution)/shard_map/ppermute | solution.py:196
  108.2 3.7 %copy-start.8 = (s32[4]{0:T(128)S(1)}, s32[4]{0:T(128)}, u32[]{:S(2)}) copy-start(s32[4]{0:T(128)} %param.11) | copy-start | bytes 52
  113.9 26.5 %collective-permute-start.5 = (f32[8,8,16,128]{3,2,1,0:T(8,128)S(1)}, f32[8,8,16,128]{3,2,1,0:T(8,128)S(1)}, u32[]{:S(2)}, u32[]{:S(2)}) collective-permute-start(f32[8,8,16,128]{3,2,1,0:T(8,128)S(1)} %get-tuple-element.36), channel_id=1, source_target_pairs={{0,4},{4,8},{8,12},{12,0},{1,5},{5,9},{9,13},{13,1},{2,6},{6,10},{... | collective-permute-start | bytes 1572872 | tf_op jit(solution)/shard_map/ppermute | solution.py:196
  137.1 31.1 %collective-permute-start.6 = (f32[8,8,16,128]{3,2,1,0:T(8,128)}, f32[8,8,16,128]{3,2,1,0:T(8,128)S(1)}, u32[]{:S(2)}, u32[]{:S(2)}) collective-permute-start(f32[8,8,16,128]{3,2,1,0:T(8,128)} %get-tuple-element.22), channel_id=1, source_target_pairs={{0,12},{4,0},{8,4},{12,8},{1,13},{5,1},{9,5},{13,9},{2,14},{6,2},{... | collective-permute-start | bytes 1572872 | tf_op jit(solution)/shard_map/ppermute | solution.py:196
  140.4 0.8 copy-start.7
  164.3 9.3 %collective-permute-start.7 = (f32[8,8,16,128]{3,2,1,0:T(8,128)}, f32[8,8,16,128]{3,2,1,0:T(8,128)S(1)}, u32[]{:S(2)}, u32[]{:S(2)}) collective-permute-start(f32[8,8,16,128]{3,2,1,0:T(8,128)} %get-tuple-element.23), channel_id=1, source_target_pairs={{0,12},{4,0},{8,4},{12,8},{1,13},{5,1},{9,5},{13,9},{2,14},{6,2},{... | collective-permute-start | bytes 1572872 | tf_op jit(solution)/shard_map/ppermute | solution.py:196
  164.4 62.3 %collective-permute-start.8 = (f32[8,8,16,128]{3,2,1,0:T(8,128)}, f32[8,8,16,128]{3,2,1,0:T(8,128)S(1)}, u32[]{:S(2)}, u32[]{:S(2)}) collective-permute-start(f32[8,8,16,128]{3,2,1,0:T(8,128)} %get-tuple-element.24), channel_id=1, source_target_pairs={{0,8},{4,12},{8,0},{12,4},{1,9},{5,13},{9,1},{13,5},{2,10},{6,14},... | collective-permute-start | bytes 1572872 | tf_op jit(solution)/shard_map/ppermute | solution.py:196
  164.5 73.8 %collective-permute-start.9 = (f32[8,8,16,128]{3,2,1,0:T(8,128)}, f32[8,8,16,128]{3,2,1,0:T(8,128)S(1)}, u32[]{:S(2)}, u32[]{:S(2)}) collective-permute-start(f32[8,8,16,128]{3,2,1,0:T(8,128)} %get-tuple-element.25), channel_id=1, source_target_pairs={{0,8},{4,12},{8,0},{12,4},{1,9},{5,13},{9,1},{13,5},{2,10},{6,14},... | collective-permute-start | bytes 1572872 | tf_op jit(solution)/shard_map/ppermute | solution.py:196
  166.8 71.5 %collective-permute-start.10 = (f32[8,8,16,128]{3,2,1,0:T(8,128)}, f32[8,8,16,128]{3,2,1,0:T(8,128)S(1)}, u32[]{:S(2)}, u32[]{:S(2)}) collective-permute-start(f32[8,8,16,128]{3,2,1,0:T(8,128)} %get-tuple-element.26), channel_id=1, source_target_pairs={{0,4},{4,8},{8,12},{12,0},{1,5},{5,9},{9,13},{13,1},{2,6},{6,10},{... | collective-permute-start | bytes 1572872 | tf_op jit(solution)/shard_map/ppermute | solution.py:196
  168.2 70.1 %copy-start.1 = (f32[8,8,16,128]{3,2,1,0:T(8,128)}, f32[8,8,16,128]{3,2,1,0:T(8,128)S(1)}, u32[]{:S(2)}) copy-start(f32[8,8,16,128]{3,2,1,0:T(8,128)S(1)} %collective-permute-done.6) | copy-start | bytes 1572868
  168.2 70.1 %collective-permute-start.11 = (f32[8,8,16,128]{3,2,1,0:T(8,128)}, f32[8,8,16,128]{3,2,1,0:T(8,128)S(1)}, u32[]{:S(2)}, u32[]{:S(2)}) collective-permute-start(f32[8,8,16,128]{3,2,1,0:T(8,128)} %get-tuple-element.27), channel_id=1, source_target_pairs={{0,4},{4,8},{8,12},{12,0},{1,5},{5,9},{9,13},{13,1},{2,6},{6,10},{... | collective-permute-start | bytes 1572872 | tf_op jit(solution)/shard_map/ppermute | solution.py:196
  173.6 64.7 %copy-start.2 = (f32[8,8,16,128]{3,2,1,0:T(8,128)}, f32[8,8,16,128]{3,2,1,0:T(8,128)S(1)}, u32[]{:S(2)}) copy-start(f32[8,8,16,128]{3,2,1,0:T(8,128)S(1)} %collective-permute-done.7) | copy-start | bytes 1572868
  226.7 11.6 %copy-start.3 = (f32[8,8,16,128]{3,2,1,0:T(8,128)}, f32[8,8,16,128]{3,2,1,0:T(8,128)S(1)}, u32[]{:S(2)}) copy-start(f32[8,8,16,128]{3,2,1,0:T(8,128)S(1)} %collective-permute-done.8) | copy-start | bytes 1572868
  238.3 0.8 copy-start.4
  238.3 1.0 copy-start.5
  238.3 1.2 copy-start.6
  264.4 30.7 %collective-permute-start.12 = (f32[32,64,128]{2,1,0:T(8,128)}, f32[32,64,128]{2,1,0:T(8,128)S(1)}, u32[]{:S(2)}, u32[]{:S(2)}) collective-permute-start(f32[32,64,128]{2,1,0:T(8,128)} %get-tuple-element.34), channel_id=1, source_target_pairs={{0,1},{1,2},{2,3},{3,0},{4,5},{5,6},{6,7},{7,4},{8,9},{9,10},{10,1... | collective-permute-start | bytes 3145736 | tf_op jit(solution)/shard_map/ppermute | solution.py:196
  272.1 46.2 %collective-permute-start.13 = (f32[32,64,128]{2,1,0:T(8,128)S(1)}, f32[32,64,128]{2,1,0:T(8,128)}, u32[]{:S(2)}, u32[]{:S(2)}) collective-permute-start(f32[32,64,128]{2,1,0:T(8,128)S(1)} %get-tuple-element.33), channel_id=1, source_target_pairs={{0,2},{1,3},{2,0},{3,1},{4,6},{5,7},{6,4},{7,5},{8,10},{9,11},{10,... | collective-permute-start | bytes 3145736 | tf_op jit(solution)/shard_map/ppermute | solution.py:196
  272.4 46.2 %collective-permute-start.14 = (f32[32,64,128]{2,1,0:T(8,128)S(1)}, f32[32,64,128]{2,1,0:T(8,128)}, u32[]{:S(2)}, u32[]{:S(2)}) collective-permute-start(f32[32,64,128]{2,1,0:T(8,128)S(1)} %get-tuple-element.32), channel_id=1, source_target_pairs={{0,3},{1,0},{2,1},{3,2},{4,7},{5,4},{6,5},{7,6},{8,11},{9,8},{10,9... | collective-permute-start | bytes 3145736 | tf_op jit(solution)/shard_map/ppermute | solution.py:196
  295.1 23.5 %copy-start = (f32[32,64,128]{2,1,0:T(8,128)}, f32[32,64,128]{2,1,0:T(8,128)S(1)}, u32[]{:S(2)}) copy-start(f32[32,64,128]{2,1,0:T(8,128)S(1)} %collective-permute-done.12.refs_1_) | copy-start | bytes 3145732
  325.1 2.0 collective-permute-start.15
  325.1 4.0 %collective-permute-start.16 = (f32[64,256]{1,0:T(8,128)S(1)}, f32[64,256]{1,0:T(8,128)S(1)}, u32[]{:S(2)}, u32[]{:S(2)}) collective-permute-start(f32[64,256]{1,0:T(8,128)S(1)} %get-tuple-element.46), channel_id=1, source_target_pairs={{0,2},{1,3},{2,0},{3,1},{4,6},{5,7},{6,4},{7,5},{8,10},{9,11},{10,... | collective-permute-start | bytes 196616 | tf_op jit(solution)/shard_map/ppermute | solution.py:196
  326.4 3.7 %collective-permute-start.17 = (f32[64,256]{1,0:T(8,128)S(1)}, f32[64,256]{1,0:T(8,128)S(1)}, u32[]{:S(2)}, u32[]{:S(2)}) collective-permute-start(f32[64,256]{1,0:T(8,128)S(1)} %get-tuple-element.45), channel_id=1, source_target_pairs={{0,3},{1,0},{2,1},{3,2},{4,7},{5,4},{6,5},{7,6},{8,11},{9,8},{10,9... | collective-permute-start | bytes 196616 | tf_op jit(solution)/shard_map/ppermute | solution.py:196
  331.0 5.6 %collective-permute-start.18 = (f32[64,256]{1,0:T(8,128)S(1)}, f32[64,256]{1,0:T(8,128)S(1)}, u32[]{:S(2)}, u32[]{:S(2)}) collective-permute-start(f32[64,256]{1,0:T(8,128)S(1)} %add_add_fusion), channel_id=1, source_target_pairs={{0,4},{4,8},{8,12},{12,0},{1,5},{5,9},{9,13},{13,1},{2,6},{6,10},{... | collective-permute-start | bytes 196616 | tf_op jit(solution)/shard_map/ppermute | solution.py:196
  331.2 5.3 %collective-permute-start.19 = (f32[64,256]{1,0:T(8,128)S(1)}, f32[64,256]{1,0:T(8,128)S(1)}, u32[]{:S(2)}, u32[]{:S(2)}) collective-permute-start(f32[64,256]{1,0:T(8,128)S(1)} %add_add_fusion), channel_id=1, source_target_pairs={{0,8},{4,12},{8,0},{12,4},{1,9},{5,13},{9,1},{13,5},{2,10},{6,14},... | collective-permute-start | bytes 196616 | tf_op jit(solution)/shard_map/ppermute | solution.py:196
  333.1 5.3 %collective-permute-start.20 = (f32[64,256]{1,0:T(8,128)S(1)}, f32[64,256]{1,0:T(8,128)S(1)}, u32[]{:S(2)}, u32[]{:S(2)}) collective-permute-start(f32[64,256]{1,0:T(8,128)S(1)} %add_add_fusion), channel_id=1, source_target_pairs={{0,12},{4,0},{8,4},{12,8},{1,13},{5,1},{9,5},{13,9},{2,14},{6,2},{... | collective-permute-start | bytes 196616 | tf_op jit(solution)/shard_map/ppermute | solution.py:196
Sparse Core Ops, SparseCore 0:
  111.6 53.1 all-reduce.3
